TPU v7x, 512 devices: a whole 4x4x16 slice. The times are simulated.
512 devices in a mesh: gx: 16 (over z_hi, x), gy: 32 (over y, z_lo, core).
Axes of the slice: x: 4, y: 4, z: 16 (z_hi: 4, z_lo: 4; z = z_hi * 4 + z_lo), core: 2. Of those that a mesh axis runs over, the one named last changes fastest.
Arguments:
- features: bfloat16 [16, 32, 1, 8, 8, 8, 128], P('gx', 'gy'), may hold values from -6 to 6
- pre_acts: bfloat16 [2, 16, 32, 1, 8, 8, 8, 128], P(None, 'gx', 'gy'), may hold values from -6 to 6
- cotangent: bfloat16 [16, 32, 1, 8, 8, 8, 128], P('gx', 'gy'), may hold values from -6 to 6
- weights: bfloat16 [2, 27, 128, 128], replicated, may hold values from -0.109375 to 0.109375
- voxel_mask: int32 [16, 32, 1, 512], P('gx', 'gy'), may hold values from 0 to 1, as said below
- neighbours: int32 [16, 32, 1, 27], P('gx', 'gy'), may hold values from -1 to 8, as said below
Outputs:
- grad_input: bfloat16 [16, 32, 1, 8, 8, 8, 128], P('gx', 'gy')
- weight_grads: bfloat16 [2, 27, 128, 128], replicated
Inputs may be any that keep to these rules, and one draw needn't show every extreme that they name: `neighbours`: the map is cut into block columns, one a device, each a column of 2 tile positions along the height; the active positions of a block column occupy its first slots in order of height, and the other slots are empty. Entry k of a slot's list names the active tile displaced by (a, b, c) tiles, as (3 (a + 1) + (b + 1)) + its slot on the owning device, or -1 where that position is inactive or off the map; an active tile's entry 13 names itself, all entries of an empty slot are -1, and the lists are symmetric. Every device holds exactly one active tile; both ends of the range are reached. `voxel_mask`: 1 marks an occupied voxel; empty tile slots are all zero.
All inputs are finite; a program needn't handle non-finite values.
Results may differ from a plain program's by a relative error of at most 0.0049.
Values may be sent and summed in bfloat16 or wider, within the bound.
A program may use at most 128 MiB of HBM per device.

v0:
```python
import math

import jax
import jax.numpy as jnp
from jax import lax
from jax.sharding import PartitionSpec as P


def extended(block, sides, width):
    for axis, dim in sides:
        count = lax.axis_size(axis)
        forward = [(i, i + 1) for i in range(count - 1)]
        backward = [(target, source) for source, target in forward]
        low = lax.ppermute(
            lax.slice_in_dim(block, block.shape[dim] - width, None, axis=dim), axis, forward
        )
        high = lax.ppermute(lax.slice_in_dim(block, 0, width, axis=dim), axis, backward)
        block = jnp.concatenate([low, block, high], axis=dim)
    return block


def rim_slice(offset):
    if offset < 0:
        return slice(7, 8)
    if offset > 0:
        return slice(0, 1)
    return slice(0, 8)


def assemble(source, lookup):
    planes = []
    for a in (-1, 0, 1):
        y_parts = []
        for b in (-1, 0, 1):
            z_parts = []
            for c in (-1, 0, 1):
                k = (a + 1) * 9 + (b + 1) * 3 + (c + 1)
                rim_part = source[:, rim_slice(a), rim_slice(b), rim_slice(c)]
                z_parts.append(jnp.take(rim_part, lookup[:, k], axis=0))
            y_parts.append(jnp.concatenate(z_parts, axis=3))
        planes.append(jnp.concatenate(y_parts, axis=2))
    return jnp.concatenate(planes, axis=1)


def patch_matrix(padded, channels, sign):
    windows = []
    for a in (-1, 0, 1):
        for b in (-1, 0, 1):
            for c in (-1, 0, 1):
                windows.append(
                    padded[
                        :,
                        1 + sign * a : 9 + sign * a,
                        1 + sign * b : 9 + sign * b,
                        1 + sign * c : 9 + sign * c,
                    ].reshape(-1, channels)
                )
    return jnp.concatenate(windows, axis=1)


def weight_terms(padded_in, out_grad, channels):
    flat_grad = out_grad.reshape(-1, channels)
    patches = patch_matrix(padded_in, channels, 1)
    product = lax.dot_general(
        patches, flat_grad, (((0,), (0,)), ((), ())), preferred_element_type=jnp.float32
    )
    return product.reshape(27, channels, channels)


def input_terms(padded_grad, kernels, channels):
    tile_total = padded_grad.shape[0]
    patches = patch_matrix(padded_grad, channels, -1)
    stacked_kernels = jnp.transpose(kernels, (0, 2, 1)).reshape(27 * channels, channels)
    running = jnp.dot(patches, stacked_kernels, preferred_element_type=jnp.float32)
    return running.reshape(tile_total, 8, 8, 8, channels)


def on_device(features, pre_acts, cotangent, weights, voxel_mask, neighbours):
    layer_count = pre_acts.shape[0]
    tile_count = features.shape[2]
    channels = features.shape[-1]
    voxel_on = voxel_mask.reshape(tile_count, 8, 8, 8, 1) > 0
    zero_value = jnp.zeros((), jnp.bfloat16)
    zero_tile = jnp.zeros((1, 8, 8, 8, channels), jnp.bfloat16)
    listed = neighbours.reshape(tile_count, 27)
    lookup = jnp.where(listed < 0, 9 * tile_count, listed)
    pre_flat = pre_acts.reshape(layer_count, tile_count, 8, 8, 8, channels)
    first = features.reshape(1, tile_count, 8, 8, 8, channels)
    stacked = jnp.concatenate([first, jnp.maximum(pre_flat[: layer_count - 1], zero_value)], axis=0)
    inputs = jnp.where(voxel_on, stacked, zero_value)
    sectioned = inputs.reshape(layer_count, 1, 1, tile_count, 8, 8, 8, channels)
    gathered = extended(sectioned, (("gx", 1), ("gy", 2)), 1)
    gathered = gathered.reshape(layer_count, 9 * tile_count, 8, 8, 8, channels)
    out_grad = jnp.where(
        voxel_on & (pre_flat[layer_count - 1] > 0),
        cotangent.reshape(tile_count, 8, 8, 8, channels),
        zero_value,
    )
    device_total = lax.axis_size("gx") * lax.axis_size("gy")
    norm_scale = 1.0 / math.sqrt(device_total * tile_count * 512)
    collected = [None] * layer_count
    grad_input = None
    for layer_no in reversed(range(layer_count)):
        padded_in = assemble(jnp.concatenate([gathered[layer_no], zero_tile], axis=0), lookup)
        kernel_sums = weight_terms(padded_in, out_grad, channels)
        summed = lax.psum(kernel_sums, ("gx", "gy"))
        collected[layer_no] = (summed * norm_scale).astype(jnp.bfloat16)
        grad_block = out_grad.reshape(1, 1, tile_count, 8, 8, 8, channels)
        beside_all = extended(grad_block, (("gx", 0), ("gy", 1)), 1)
        beside_all = beside_all.reshape(9 * tile_count, 8, 8, 8, channels)
        padded_grad = assemble(jnp.concatenate([beside_all, zero_tile], axis=0), lookup)
        grad_in = input_terms(padded_grad, weights[layer_no], channels)
        if layer_no > 0:
            out_grad = jnp.where(voxel_on & (pre_flat[layer_no - 1] > 0), grad_in, 0.0).astype(
                jnp.bfloat16
            )
        else:
            grad_input = jnp.where(voxel_on, grad_in, 0.0).astype(jnp.bfloat16)
    weight_grads = jnp.stack(collected)
    return (grad_input.reshape(1, 1, tile_count, 8, 8, 8, channels), weight_grads)


def solution(mesh):
    in_specs = (
        P("gx", "gy", None, None, None, None, None),
        P(None, "gx", "gy", None, None, None, None, None),
        P("gx", "gy", None, None, None, None, None),
        P(),
        P("gx", "gy", None, None),
        P("gx", "gy", None, None),
    )
    out_specs = (P("gx", "gy", None, None, None, None, None), P())
    return jax.shard_map(
        on_device, mesh=mesh, in_specs=in_specs, out_specs=out_specs, check_vma=False
    )
```

profile of v0, /device:TPU:1, one launch (start us, length us, event | category | flops | bytes accessed | tf_op | source)
XLA Modules:
  0.0 784.2 jit_solution(15620308781596981119)
XLA Ops:
  8.1 1.1 fusion.5
  9.2 1.3 collective-permute-start.1
  10.5 4.6 collective-permute-start
  67.1 8.7 %collective-permute-start.3 = (bf16[3,1,1,8,8,8,128]{6,5,4,3,2,1,0:T(8,128)(2,1)}, bf16[3,1,1,8,8,8,128]{6,5,4,3,2,1,0:T(8,128)(2,1)}, u32[]{:S(2)}, u32[]{:S(2)}) collective-permute-start(bf16[3,1,1,8,8,8,128]{6,5,4,3,2,1,0:T(8,128)(2,1)} %pad_maximum_fusion.5), channel_id=1, source_target_pairs={{1,0},{2,1},{3,2},{4,3},{5,4},{6,5},{7,6},{8,7},{9,8},{10,9},{11,1... | collective-permute-start | bytes 1179656 | tf_op jit(solution)/shard_map/ppermute | solution.py:17
  75.9 1.9 collective-permute-start.2
  77.8 1.6 slice_bitcast_fusion
  79.3 1.3 copy.8
  80.8 2.0 collective-permute-done.2
  82.8 1.2 pad_maximum_fusion.2
  88.1 1.1 fusion
  89.2 1.3 collective-permute-start.5
  90.5 4.0 collective-permute-start.4
  94.6 1.3 collective-permute-start.9
  95.9 4.0 collective-permute-start.8
  100.8 2.3 collective-permute-start.7
  103.1 5.1 collective-permute-start.6
  108.2 1.3 copy.9
  109.6 1.9 collective-permute-start.11
  111.6 3.6 collective-permute-start.10
  115.2 1.1 pad_maximum_fusion.3
  117.4 9.4 %collective-permute-done.11 = bf16[2,3,1,1,8,8,8,128]{7,6,5,4,3,2,1,0:T(8,128)(2,1)S(1)} collective-permute-done((bf16[2,3,1,1,8,8,8,128]{7,6,5,4,3,2,1,0:T(8,128)(2,1)S(1)}, bf16[2,3,1,1,8,8,8,128]{7,6,5,4,3,2,1,0:T(8,128)(2,1)S(1)}, u32[]{:S(2)}, u32[]{:S(2)}) %collective-permute-start.11) | collective-permute-done | bytes 786464 | tf_op jit(solution)/shard_map/ppermute | solution.py:17
  127.8 0.9 pad_slice_fusion.16
  129.4 1.7 pad_slice_fusion.13
  133.2 0.9 pad_slice_fusion.5
  138.1 0.9 broadcast_select_fusion.40
  141.4 0.9 fusion.46
  142.2 1.7 copy.37
  143.9 1.6 constant_dynamic-update-slice_fusion.107
  145.5 1.7 copy.38
  147.1 1.7 copy.39
  164.1 1.2 broadcast_select_fusion.56
  165.3 1.1 broadcast_select_fusion.60
  166.4 1.2 broadcast_select_fusion.64
  185.6 0.8 fusion.44
  186.4 1.7 copy.10
  188.1 1.6 constant_dynamic-update-slice_fusion.80
  189.6 1.6 copy.11
  214.9 1.7 constant_dynamic-update-slice_fusion.106
  216.6 1.6 constant_dynamic-update-slice_fusion.105
  218.2 1.6 constant_dynamic-update-slice_fusion.104
  219.7 1.6 constant_dynamic-update-slice_fusion.103
  224.0 1.6 constant_dynamic-update-slice_fusion.98
  237.0 4.4 fusion.54
  242.7 2.3 fusion.53
  250.2 3.7 fusion.2
  253.9 519.8 %all-reduce.7.cloned.1.call-done = (f32[27,128,128]{2,1,0:T(8,128)}, f32[27,128,128]{2,1,0:T(8,128)}) async-done(((f32[27,128,128]{2,1,0:T(8,128)}, f32[27,128,128]{2,1,0:T(8,128)}), (f32[27,128,128]{2,1,0:T(8,128)}, f32[27,128,128]{2,1,0:T(8,128)})) %all-reduce.7.cloned.1.call-update) | async-done | bytes 3538960 | tf_op jit(solution)/shard_map/psum | solution.py:106
  773.7 1.8 fusion.4
  776.0 1.4 pad_maximum_fusion.1
  (414 shorter events, 96.4 us)
Async XLA Ops:
  7.2 73.6 %copy-start.3 = (bf16[2,1,1,1,8,8,8,128]{7,6,5,4,3,2,1,0:T(8,128)(2,1)S(1)}, bf16[2,1,1,1,8,8,8,128]{7,6,5,4,3,2,1,0:T(8,128)(2,1)}, u32[]{:S(2)}) copy-start(bf16[2,1,1,1,8,8,8,128]{7,6,5,4,3,2,1,0:T(8,128)(2,1)} %param.23) | copy-start | bytes 786436
  7.2 766.6 %all-reduce.7.cloned.1.call-start = ((), (), s32[]{:S(2)}) async-start(), calls=%async_computation | async-start | bytes 7077888 | tf_op jit(solution)/shard_map/psum | solution.py:106
  9.2 57.1 %collective-permute-start.1 = (bf16[1,1,1,8,8,8,128]{6,5,4,3,2,1,0:T(8,128)(2,1)S(1)}, bf16[1,1,1,8,8,8,128]{6,5,4,3,2,1,0:T(8,128)(2,1)S(1)}, u32[]{:S(2)}, u32[]{:S(2)}) collective-permute-start(bf16[1,1,1,8,8,8,128]{6,5,4,3,2,1,0:T(8,128)(2,1)S(1)} %fusion.5), channel_id=1, source_target_pairs={{32,0},{64,32},{96,64},{128,96},{160,128},{192,160},{224,192},{256... | collective-permute-start | bytes 393224 | tf_op jit(solution)/shard_map/ppermute | solution.py:17
  10.5 55.8 %collective-permute-start = (bf16[1,1,1,8,8,8,128]{6,5,4,3,2,1,0:T(8,128)(2,1)S(1)}, bf16[1,1,1,8,8,8,128]{6,5,4,3,2,1,0:T(8,128)(2,1)S(1)}, u32[]{:S(2)}, u32[]{:S(2)}) collective-permute-start(bf16[1,1,1,8,8,8,128]{6,5,4,3,2,1,0:T(8,128)(2,1)S(1)} %fusion.5), channel_id=1, source_target_pairs={{0,32},{32,64},{64,96},{96,128},{128,160},{160,192},{192,224},{224... | collective-permute-start | bytes 393224 | tf_op jit(solution)/shard_map/ppermute | solution.py:14
  67.1 13.7 %collective-permute-start.3 = (bf16[3,1,1,8,8,8,128]{6,5,4,3,2,1,0:T(8,128)(2,1)}, bf16[3,1,1,8,8,8,128]{6,5,4,3,2,1,0:T(8,128)(2,1)}, u32[]{:S(2)}, u32[]{:S(2)}) collective-permute-start(bf16[3,1,1,8,8,8,128]{6,5,4,3,2,1,0:T(8,128)(2,1)} %pad_maximum_fusion.5), channel_id=1, source_target_pairs={{1,0},{2,1},{3,2},{4,3},{5,4},{6,5},{7,6},{8,7},{9,8},{10,9},{11,1... | collective-permute-start | bytes 1179656 | tf_op jit(solution)/shard_map/ppermute | solution.py:17
  75.9 6.9 collective-permute-start.2
  87.5 7.0 copy-start.51
  89.2 10.8 %collective-permute-start.5 = (bf16[1,1,1,8,8,8,128]{6,5,4,3,2,1,0:T(8,128)(2,1)S(1)}, bf16[1,1,1,8,8,8,128]{6,5,4,3,2,1,0:T(8,128)(2,1)S(1)}, u32[]{:S(2)}, u32[]{:S(2)}) collective-permute-start(bf16[1,1,1,8,8,8,128]{6,5,4,3,2,1,0:T(8,128)(2,1)S(1)} %bitcast.610), channel_id=1, source_target_pairs={{32,0},{64,32},{96,64},{128,96},{160,128},{192,160},{224,192},{256... | collective-permute-start | bytes 393224 | tf_op jit(solution)/shard_map/ppermute | solution.py:17
  90.5 9.5 %collective-permute-start.4 = (bf16[1,1,1,8,8,8,128]{6,5,4,3,2,1,0:T(8,128)(2,1)S(1)}, bf16[1,1,1,8,8,8,128]{6,5,4,3,2,1,0:T(8,128)(2,1)S(1)}, u32[]{:S(2)}, u32[]{:S(2)}) collective-permute-start(bf16[1,1,1,8,8,8,128]{6,5,4,3,2,1,0:T(8,128)(2,1)S(1)} %bitcast.611), channel_id=1, source_target_pairs={{0,32},{32,64},{64,96},{96,128},{128,160},{160,192},{192,224},{224... | collective-permute-start | bytes 393224 | tf_op jit(solution)/shard_map/ppermute | solution.py:14
  94.6 14.9 %collective-permute-start.9 = (bf16[2,1,1,1,8,8,8,128]{7,6,5,4,3,2,1,0:T(8,128)(2,1)S(1)}, bf16[2,1,1,1,8,8,8,128]{7,6,5,4,3,2,1,0:T(8,128)(2,1)S(1)}, u32[]{:S(2)}, u32[]{:S(2)}) collective-permute-start(bf16[2,1,1,1,8,8,8,128]{7,6,5,4,3,2,1,0:T(8,128)(2,1)S(1)} %maximum_select_fusion), channel_id=1, source_target_pairs={{32,0},{64,32},{96,64},{128,96},{160,128},{192,160},{224,192},{256... | collective-permute-start | bytes 786440 | tf_op jit(solution)/shard_map/ppermute | solution.py:17
  95.9 13.6 %collective-permute-start.8 = (bf16[2,1,1,1,8,8,8,128]{7,6,5,4,3,2,1,0:T(8,128)(2,1)S(1)}, bf16[2,1,1,1,8,8,8,128]{7,6,5,4,3,2,1,0:T(8,128)(2,1)S(1)}, u32[]{:S(2)}, u32[]{:S(2)}) collective-permute-start(bf16[2,1,1,1,8,8,8,128]{7,6,5,4,3,2,1,0:T(8,128)(2,1)S(1)} %maximum_select_fusion), channel_id=1, source_target_pairs={{0,32},{32,64},{64,96},{96,128},{128,160},{160,192},{192,224},{224... | collective-permute-start | bytes 786440 | tf_op jit(solution)/shard_map/ppermute | solution.py:14
  100.8 14.5 %collective-permute-start.7 = (bf16[3,1,1,8,8,8,128]{6,5,4,3,2,1,0:T(8,128)(2,1)}, bf16[3,1,1,8,8,8,128]{6,5,4,3,2,1,0:T(8,128)(2,1)S(1)}, u32[]{:S(2)}, u32[]{:S(2)}) collective-permute-start(bf16[3,1,1,8,8,8,128]{6,5,4,3,2,1,0:T(8,128)(2,1)} %pad_maximum_fusion.6), channel_id=1, source_target_pairs={{1,0},{2,1},{3,2},{4,3},{5,4},{6,5},{7,6},{8,7},{9,8},{10,9},{11,1... | collective-permute-start | bytes 1179656 | tf_op jit(solution)/shard_map/ppermute | solution.py:17
  103.1 12.1 %collective-permute-start.6 = (bf16[3,1,1,8,8,8,128]{6,5,4,3,2,1,0:T(8,128)(2,1)}, bf16[3,1,1,8,8,8,128]{6,5,4,3,2,1,0:T(8,128)(2,1)}, u32[]{:S(2)}, u32[]{:S(2)}) collective-permute-start(bf16[3,1,1,8,8,8,128]{6,5,4,3,2,1,0:T(8,128)(2,1)} %pad_maximum_fusion.6), channel_id=1, source_target_pairs={{0,1},{1,2},{2,3},{3,4},{4,5},{5,6},{6,7},{7,8},{8,9},{9,10},{10,1... | collective-permute-start | bytes 1179656 | tf_op jit(solution)/shard_map/ppermute | solution.py:14
  109.6 17.1 %collective-permute-start.11 = (bf16[2,3,1,1,8,8,8,128]{7,6,5,4,3,2,1,0:T(8,128)(2,1)S(1)}, bf16[2,3,1,1,8,8,8,128]{7,6,5,4,3,2,1,0:T(8,128)(2,1)S(1)}, u32[]{:S(2)}, u32[]{:S(2)}) collective-permute-start(bf16[2,3,1,1,8,8,8,128]{7,6,5,4,3,2,1,0:T(8,128)(2,1)S(1)} %pad_maximum_fusion.4), channel_id=1, source_target_pairs={{1,0},{2,1},{3,2},{4,3},{5,4},{6,5},{7,6},{8,7},{9,8},{10,9},{11,1... | collective-permute-start | bytes 2359304 | tf_op jit(solution)/shard_map/ppermute | solution.py:17
  111.6 15.2 %collective-permute-start.10 = (bf16[2,3,1,1,8,8,8,128]{7,6,5,4,3,2,1,0:T(8,128)(2,1)S(1)}, bf16[2,3,1,1,8,8,8,128]{7,6,5,4,3,2,1,0:T(8,128)(2,1)S(1)}, u32[]{:S(2)}, u32[]{:S(2)}) collective-permute-start(bf16[2,3,1,1,8,8,8,128]{7,6,5,4,3,2,1,0:T(8,128)(2,1)S(1)} %pad_maximum_fusion.4), channel_id=1, source_target_pairs={{0,1},{1,2},{2,3},{3,4},{4,5},{5,6},{6,7},{7,8},{8,9},{9,10},{10,1... | collective-permute-start | bytes 2359304 | tf_op jit(solution)/shard_map/ppermute | solution.py:14
  162.7 22.6 %copy-start.52 = (bf16[1,1,1,1,128]{4,3,2,1,0:T(2,128)(2,1)S(1)}, bf16[1,1,1,1,128]{4,3,2,1,0:T(2,128)(2,1)}, u32[]{:S(2)}) copy-start(bf16[1,1,1,1,128]{4,3,2,1,0:T(2,128)(2,1)} %get-tuple-element.350) | copy-start | bytes 772
  162.7 22.6 %copy-start.53 = (bf16[1,1,1,1,128]{4,3,2,1,0:T(2,128)(2,1)S(1)}, bf16[1,1,1,1,128]{4,3,2,1,0:T(2,128)(2,1)}, u32[]{:S(2)}) copy-start(bf16[1,1,1,1,128]{4,3,2,1,0:T(2,128)(2,1)} %get-tuple-element.352) | copy-start | bytes 772
  162.7 22.6 %copy-start.54 = (bf16[1,1,1,1,128]{4,3,2,1,0:T(2,128)(2,1)S(1)}, bf16[1,1,1,1,128]{4,3,2,1,0:T(2,128)(2,1)}, u32[]{:S(2)}) copy-start(bf16[1,1,1,1,128]{4,3,2,1,0:T(2,128)(2,1)} %get-tuple-element.354) | copy-start | bytes 772
  162.7 22.6 %copy-start.56 = (bf16[1,1,1,1,128]{4,3,2,1,0:T(2,128)(2,1)S(1)}, bf16[1,1,1,1,128]{4,3,2,1,0:T(2,128)(2,1)}, u32[]{:S(2)}) copy-start(bf16[1,1,1,1,128]{4,3,2,1,0:T(2,128)(2,1)} %get-tuple-element.356) | copy-start | bytes 772
  186.4 20.8 %copy-start.55 = (bf16[1,1,1,1,128]{4,3,2,1,0:T(2,128)(2,1)S(1)}, bf16[1,1,1,1,128]{4,3,2,1,0:T(2,128)(2,1)}, u32[]{:S(2)}) copy-start(bf16[1,1,1,1,128]{4,3,2,1,0:T(2,128)(2,1)} %get-tuple-element.296) | copy-start | bytes 772
  186.4 20.8 %copy-start.57 = (bf16[1,1,1,1,128]{4,3,2,1,0:T(2,128)(2,1)S(1)}, bf16[1,1,1,1,128]{4,3,2,1,0:T(2,128)(2,1)}, u32[]{:S(2)}) copy-start(bf16[1,1,1,1,128]{4,3,2,1,0:T(2,128)(2,1)} %get-tuple-element.330) | copy-start | bytes 772
  186.4 20.8 %copy-start.58 = (bf16[1,1,1,1,128]{4,3,2,1,0:T(2,128)(2,1)S(1)}, bf16[1,1,1,1,128]{4,3,2,1,0:T(2,128)(2,1)}, u32[]{:S(2)}) copy-start(bf16[1,1,1,1,128]{4,3,2,1,0:T(2,128)(2,1)} %get-tuple-element.338) | copy-start | bytes 772
  202.2 19.1 %copy-start.9 = (bf16[512,128]{0,1:T(8,128)(2,1)S(1)}, bf16[512,128]{0,1:T(8,128)(2,1)}, u32[]{:S(2)}) copy-start(bf16[512,128]{0,1:T(8,128)(2,1)} %copy.42) | copy-start | bytes 393220
  203.0 19.0 %copy-start.7 = (bf16[512,128]{0,1:T(8,128)(2,1)S(1)}, bf16[512,128]{0,1:T(8,128)(2,1)}, u32[]{:S(2)}) copy-start(bf16[512,128]{0,1:T(8,128)(2,1)} %copy.43) | copy-start | bytes 393220
  203.8 18.9 %copy-start.4 = (bf16[512,128]{0,1:T(8,128)(2,1)S(1)}, bf16[512,128]{0,1:T(8,128)(2,1)}, u32[]{:S(2)}) copy-start(bf16[512,128]{0,1:T(8,128)(2,1)} %copy.44) | copy-start | bytes 393220
  207.3 16.1 %copy-start.5 = (bf16[512,128]{0,1:T(8,128)(2,1)S(1)}, bf16[512,128]{0,1:T(8,128)(2,1)}, u32[]{:S(2)}) copy-start(bf16[512,128]{0,1:T(8,128)(2,1)} %copy.45) | copy-start | bytes 393220
  207.7 19.8 %copy-start.8 = (bf16[512,128]{0,1:T(8,128)(2,1)S(1)}, bf16[512,128]{0,1:T(8,128)(2,1)}, u32[]{:S(2)}) copy-start(bf16[512,128]{0,1:T(8,128)(2,1)} %copy.50) | copy-start | bytes 393220
  207.7 20.5 %copy-start.6 = (bf16[512,128]{0,1:T(8,128)(2,1)S(1)}, bf16[512,128]{0,1:T(8,128)(2,1)}, u32[]{:S(2)}) copy-start(bf16[512,128]{0,1:T(8,128)(2,1)} %copy.51) | copy-start | bytes 393220
  208.7 18.1 %copy-start.10 = (bf16[512,128]{0,1:T(8,128)(2,1)S(1)}, bf16[512,128]{0,1:T(8,128)(2,1)}, u32[]{:S(2)}) copy-start(bf16[512,128]{0,1:T(8,128)(2,1)} %copy.49) | copy-start | bytes 393220
  209.5 16.0 %copy-start.11 = (bf16[512,128]{0,1:T(8,128)(2,1)S(1)}, bf16[512,128]{0,1:T(8,128)(2,1)}, u32[]{:S(2)}) copy-start(bf16[512,128]{0,1:T(8,128)(2,1)} %copy.47) | copy-start | bytes 393220
  210.3 15.9 %copy-start.12 = (bf16[512,128]{0,1:T(8,128)(2,1)S(1)}, bf16[512,128]{0,1:T(8,128)(2,1)}, u32[]{:S(2)}) copy-start(bf16[512,128]{0,1:T(8,128)(2,1)} %copy.48) | copy-start | bytes 393220
  211.1 18.5 %copy-start.13 = (bf16[512,128]{0,1:T(8,128)(2,1)S(1)}, bf16[512,128]{0,1:T(8,128)(2,1)}, u32[]{:S(2)}) copy-start(bf16[512,128]{0,1:T(8,128)(2,1)} %copy.53) | copy-start | bytes 393220
  211.8 18.4 %copy-start.14 = (bf16[512,128]{0,1:T(8,128)(2,1)S(1)}, bf16[512,128]{0,1:T(8,128)(2,1)}, u32[]{:S(2)}) copy-start(bf16[512,128]{0,1:T(8,128)(2,1)} %copy.54) | copy-start | bytes 393220
  212.6 16.3 %copy-start.15 = (bf16[512,128]{0,1:T(8,128)(2,1)S(1)}, bf16[512,128]{0,1:T(8,128)(2,1)}, u32[]{:S(2)}) copy-start(bf16[512,128]{0,1:T(8,128)(2,1)} %copy.52) | copy-start | bytes 393220
  213.4 22.2 %copy-start.16 = (bf16[512,128]{0,1:T(8,128)(2,1)S(1)}, bf16[512,128]{0,1:T(8,128)(2,1)}, u32[]{:S(2)}) copy-start(bf16[512,128]{0,1:T(8,128)(2,1)} %copy.62) | copy-start | bytes 393220
  214.1 22.1 %copy-start.17 = (bf16[512,128]{0,1:T(8,128)(2,1)S(1)}, bf16[512,128]{0,1:T(8,128)(2,1)}, u32[]{:S(2)}) copy-start(bf16[512,128]{0,1:T(8,128)(2,1)} %copy.63) | copy-start | bytes 393220
  214.9 16.0 %copy-start.24 = (bf16[512,128]{0,1:T(8,128)(2,1)S(1)}, bf16[512,128]{0,1:T(8,128)(2,1)}, u32[]{:S(2)}) copy-start(bf16[512,128]{0,1:T(8,128)(2,1)} %copy.55) | copy-start | bytes 393220
  214.9 16.6 %copy-start.23 = (bf16[512,128]{0,1:T(8,128)(2,1)S(1)}, bf16[512,128]{0,1:T(8,128)(2,1)}, u32[]{:S(2)}) copy-start(bf16[512,128]{0,1:T(8,128)(2,1)} %copy.56) | copy-start | bytes 393220
  214.9 17.3 %copy-start.22 = (bf16[512,128]{0,1:T(8,128)(2,1)S(1)}, bf16[512,128]{0,1:T(8,128)(2,1)}, u32[]{:S(2)}) copy-start(bf16[512,128]{0,1:T(8,128)(2,1)} %copy.57) | copy-start | bytes 393220
  214.9 18.0 %copy-start.21 = (bf16[512,128]{0,1:T(8,128)(2,1)S(1)}, bf16[512,128]{0,1:T(8,128)(2,1)}, u32[]{:S(2)}) copy-start(bf16[512,128]{0,1:T(8,128)(2,1)} %copy.58) | copy-start | bytes 393220
  214.9 18.6 %copy-start.20 = (bf16[512,128]{0,1:T(8,128)(2,1)S(1)}, bf16[512,128]{0,1:T(8,128)(2,1)}, u32[]{:S(2)}) copy-start(bf16[512,128]{0,1:T(8,128)(2,1)} %copy.59) | copy-start | bytes 393220
  214.9 19.3 %copy-start.19 = (bf16[512,128]{0,1:T(8,128)(2,1)S(1)}, bf16[512,128]{0,1:T(8,128)(2,1)}, u32[]{:S(2)}) copy-start(bf16[512,128]{0,1:T(8,128)(2,1)} %copy.60) | copy-start | bytes 393220
  214.9 20.0 %copy-start.18 = (bf16[512,128]{0,1:T(8,128)(2,1)S(1)}, bf16[512,128]{0,1:T(8,128)(2,1)}, u32[]{:S(2)}) copy-start(bf16[512,128]{0,1:T(8,128)(2,1)} %copy.61) | copy-start | bytes 393220
  232.9 8.5 %copy-start.1 = (bf16[512,3456]{0,1:T(8,128)(2,1)S(1)}, bf16[512,3456]{0,1:T(8,128)(2,1)}, u32[]{:S(2)}) copy-start(bf16[512,3456]{0,1:T(8,128)(2,1)} %constant_dynamic-update-slice_fusion.80) | copy-start | bytes 10616836
  232.9 8.5 %copy-start.39 = (bf16[512,128]{0,1:T(8,128)(2,1)S(1)}, bf16[512,128]{0,1:T(8,128)(2,1)}, u32[]{:S(2)}) copy-start(bf16[512,128]{0,1:T(8,128)(2,1)} %copy.11) | copy-start | bytes 393220
  233.6 7.9 %copy-start.40 = (bf16[512,128]{0,1:T(8,128)(2,1)S(1)}, bf16[512,128]{0,1:T(8,128)(2,1)}, u32[]{:S(2)}) copy-start(bf16[512,128]{0,1:T(8,128)(2,1)} %copy.12) | copy-start | bytes 393220
  234.2 7.3 copy-start.35
  234.9 6.7 copy-start.32
  (24 other events, 80.1 us)
Sparse Core Ops, SparseCore 0:
  245.2 528.4 all-reduce.6
where the time goes:
time: 787 us; the launch traced here: 784 us
  waiting for transfers between devices  531 us (67%)
  local copies, waits for them, and re-layouts  97.3 us (12%)
  between operations  65.1 us (8%)
  starting transfers between devices  40.1 us (5%)
  other arithmetic  38.8 us (5%)
  matrix products  11.6 us (1%)
    psum x1, waiting for transfers between devices, on_device(): summed = lax.psum(kernel_sums, ('gx', 'gy'))  520 us
    reshape x54, local copies, waits for them, and re-layouts, patch_matrix(): windows.append(padded[:, 1 + sign * a:9 + sign * a, 1 + sign * b:9 + sign...  46 us
    unnamed x216, local copies, waits for them, and re-layouts  32.5 us
    select_n x86, other arithmetic, assemble(): z_parts.append(jnp.take(rim_part, lookup[:, k], axis=0))  24 us
    ppermute x6, starting transfers between devices, extended(): lax.ppermute(lax.slice_in_dim(block, block.shape[dim] - width, None, axis...  23.2 us
    ppermute x6, starting transfers between devices, extended(): lax.ppermute(lax.slice_in_dim(block, 0, width, axis=dim), axis, backward)  16.9 us
  transfers between devices with their start and end apart: 13, of which 3 were waited for; matrix products, arithmetic and copies ran while one was open for 2% of the time, Pallas kernels for 0%

commit v1 on v0

v1 whole, which is shorter than its diff:
```python
import jax
import jax.numpy as jnp
from jax import lax
from jax.experimental import pallas as pl
from jax.experimental.pallas import tpu as pltpu
from jax.sharding import PartitionSpec as P

F32 = jnp.float32
BF16 = jnp.bfloat16
MESH = pl.DeviceIdType.MESH
SIDES = [(a, b) for a in (-1, 0, 1) for b in (-1, 0, 1) if (a, b) != (0, 0)]
CHUNK = 112


def kernel(
    feat, pre, cot, mask, nbr, w_hbm, gin, wg,
    wv, maskv, pad, pg, xt, gface, gcorner, rface, rcorner,
    s, crecv, hsum, psend, precv, zsend, zrecv, zfin, ag,
    wsem, osem, hss, hrs, css, crs, pss, prs, zss, zrs, zas, zar, pas, par, cas, car,
):
    gx, gy = lax.axis_index("gx"), lax.axis_index("gy")
    z_hi, x = gx // 4, gx % 4
    y, z_lo, core = gy // 8, (gy // 2) % 4, gy % 2
    other = 1 - core
    plane_me = x * 4 + y
    z_me = z_hi * 4 + z_lo

    def plane_device(i):
        return {"gx": z_hi * 4 + i // 4, "gy": (i % 4) * 8 + z_lo * 2 + core}

    def z_device(i):
        return {"gx": (i // 4) * 4 + x, "gy": y * 8 + (i % 4) * 2 + core}

    core_device = {"gx": gx, "gy": gy + 1 - 2 * core}

    def side_device(a, b):
        return {"gx": (gx + a + 16) % 16, "gy": (gy + b + 32) % 32}

    barrier = pltpu.get_barrier_semaphore()
    for a, b in SIDES:
        pl.semaphore_signal(barrier, inc=1, device_id=side_device(a, b), device_id_type=MESH)
    pl.semaphore_signal(barrier, inc=1, device_id=core_device, device_id_type=MESH)

    def greet(j, carry):
        pl.semaphore_signal(barrier, inc=1, device_id=plane_device((plane_me + j) % 16), device_id_type=MESH)
        pl.semaphore_signal(barrier, inc=1, device_id=z_device((z_me + j) % 16), device_id_type=MESH)
        return carry

    lax.fori_loop(1, 16, greet, 0)
    w_copies = [pltpu.make_async_copy(w_hbm.at[l], wv.at[l], wsem.at[l]) for l in (1, 0)]
    for copy in w_copies:
        copy.start()

    rows = lax.broadcasted_iota(jnp.int32, (128, 128), 0)
    cols = lax.broadcasted_iota(jnp.int32, (128, 128), 1)
    ones = jnp.ones((128, 128), BF16)
    for r in range(4):
        line = (mask[:, r * 128 : (r + 1) * 128] > 0).astype(F32)
        spread = jnp.where(rows == cols, jnp.broadcast_to(line, (128, 128)), 0.0).astype(BF16)
        maskv[r * 128 : (r + 1) * 128] = jnp.dot(spread, ones, preferred_element_type=F32)

    def flag(a, b, c):
        return jnp.where(nbr[0, (a + 1) * 9 + (b + 1) * 3 + c + 1] >= 0, 1.0, 0.0)

    level = lax.broadcasted_iota(jnp.int32, (1, 8, 128), 1)

    def place(a, b, tile):
        low, mid, high = flag(a, b, -1), flag(a, b, 0), flag(a, b, 1)
        nx, ny = (1 if a else 8), (1 if b else 8)
        x0, y0 = {-1: 0, 0: 1, 1: 9}[a], {-1: 0, 0: 1, 1: 9}[b]
        shape = (nx, ny, 8, 128)
        below = pltpu.roll(tile, 1, 1) * jnp.where(level == 0, low, mid)
        above = pltpu.roll(tile, 7, 1) * jnp.where(level == 7, high, mid)
        pad[0, x0 : x0 + nx, y0 : y0 + ny] = below.reshape(shape)
        pad[1, x0 : x0 + nx, y0 : y0 + ny] = (tile * mid).reshape(shape)
        pad[2, x0 : x0 + nx, y0 : y0 + ny] = above.reshape(shape)

    def side_copies(l):
        copies = []
        for n, (a, b) in enumerate(SIDES):
            m = SIDES.index((-a, -b))
            if a and b:
                i, j = (a + 1) + (b + 1) // 2, (1 - a) + (1 - b) // 2
                src, dst = gcorner.at[l, i], rcorner.at[l, j]
            else:
                i = (a + 1) // 2 if a else 2 + (b + 1) // 2
                j = (1 - a) // 2 if a else 2 + (1 - b) // 2
                src, dst = gface.at[l, i], rface.at[l, j]
            copies.append(
                pltpu.make_async_remote_copy(
                    src_ref=src, dst_ref=dst, send_sem=hss.at[l, n], recv_sem=hrs.at[l, m],
                    device_id=side_device(a, b), device_id_type=MESH,
                )
            )
        return copies

    def stage(l, g):
        g4 = g.reshape(8, 8, 8, 128)
        for i, e in ((0, 0), (1, 7)):
            gface[l, i] = g4[e].reshape(64, 128).astype(BF16)
            gface[l, 2 + i] = g4[:, e].reshape(64, 128).astype(BF16)
            for j, f in ((0, 0), (1, 7)):
                cell = g4[e, f]
                gcorner[l, 2 * i + j] = jnp.concatenate([cell, cell], axis=0).astype(BF16)

    def rims(l):
        for a, b in SIDES:
            if a and b:
                place(a, b, rcorner[l, (a + 1) + (b + 1) // 2].astype(F32)[:8].reshape(1, 8, 128))
            else:
                i = (a + 1) // 2 if a else 2 + (b + 1) // 2
                place(a, b, rface[l, i].astype(F32).reshape(8, 8, 128))

    def patches():
        for k in range(27):
            a, b, c = k // 9 - 1, (k // 3) % 3 - 1, k % 3 - 1
            window = pad[1 - c, 1 - a : 9 - a, 1 - b : 9 - b]
            pg[:, k * 128 : (k + 1) * 128] = window.reshape(512, 128).astype(BF16)

    def input_grads(l):
        kernels = jnp.concatenate([wv[l, k] for k in range(27)], axis=1)
        return lax.dot_general(
            pg[:, : 27 * 128], kernels, (((1,), (1,)), ((), ())), preferred_element_type=F32
        )

    def kernel_grads(l):
        for m in range(14):
            both = jnp.dot(xt[l], pg[:, m * 256 : (m + 1) * 256], preferred_element_type=F32)
            for h in (0, 1):
                half = both[h * 64 : (h + 1) * 64]
                s[l, h, m * 128 : m * 128 + 64] = half[:, :128]
                s[l, h, m * 128 + 64 : (m + 1) * 128] = half[:, 128:]

    def core_copy(l):
        return pltpu.make_async_remote_copy(
            src_ref=s.at[l, other], dst_ref=crecv.at[l], send_sem=css.at[l], recv_sem=crs.at[l],
            device_id=core_device, device_id_type=MESH,
        )

    def plane_copy(l, j):
        peer = (plane_me + j) % 16
        return pltpu.make_async_remote_copy(
            src_ref=psend.at[l, peer], dst_ref=precv.at[l, j - 1],
            send_sem=pss.at[l, j - 1], recv_sem=prs.at[l, j - 1],
            device_id=plane_device(peer), device_id_type=MESH,
        )

    def z_copy(l, j):
        peer = (z_me + j) % 16
        return pltpu.make_async_remote_copy(
            src_ref=zsend.at[l, peer], dst_ref=zrecv.at[l, j - 1],
            send_sem=zss.at[l, j - 1], recv_sem=zrs.at[l, j - 1],
            device_id=z_device(peer), device_id_type=MESH,
        )

    def z_back(l, j):
        return pltpu.make_async_remote_copy(
            src_ref=zfin.at[l, z_me], dst_ref=zfin.at[l, z_me],
            send_sem=zas.at[l, j - 1], recv_sem=zar.at[l, j - 1],
            device_id=z_device((z_me + j) % 16), device_id_type=MESH,
        )

    def plane_back(l, j):
        return pltpu.make_async_remote_copy(
            src_ref=ag.at[l, core, plane_me], dst_ref=ag.at[l, core, plane_me],
            send_sem=pas.at[l, j - 1], recv_sem=par.at[l, j - 1],
            device_id=plane_device((plane_me + j) % 16), device_id_type=MESH,
        )

    def core_back(l, j):
        owner = (plane_me + 16 - j) % 16
        return pltpu.make_async_remote_copy(
            src_ref=ag.at[l, core, owner], dst_ref=ag.at[l, core, owner],
            send_sem=cas.at[l, j], recv_sem=car.at[l, j],
            device_id=core_device, device_id_type=MESH,
        )

    def each(first, last, act):
        def step(j, carry):
            act(j)
            return carry

        lax.fori_loop(first, last, step, 0)

    def sum_halves(l):
        core_copy(l).wait_recv()

        def chunk(j):
            i = (plane_me + j) % 16
            at = pl.ds(pl.multiple_of(i * CHUNK, CHUNK), CHUNK)
            total = s[l, core, at] + crecv[l, at]
            psend[l, i] = total.astype(BF16)
            plane_copy(l, j).start()

        each(1, 16, chunk)
        at = pl.ds(pl.multiple_of(plane_me * CHUNK, CHUNK), CHUNK)
        hsum[l] = s[l, core, at] + crecv[l, at]

    def sum_plane(l):
        def add(j, total):
            plane_copy(l, j).wait_recv()
            return total + precv[l, j - 1].astype(F32)

        total = lax.fori_loop(1, 16, add, hsum[l])
        zsend[l, :14] = total.reshape(14, 8, 128)
        zsend[l, 14:] = jnp.zeros((2, 8, 128), F32)
        each(1, 16, lambda j: z_copy(l, j).start())

    def sum_z(l):
        def add(j, total):
            z_copy(l, j).wait_recv()
            return total + zrecv[l, j - 1]

        total = lax.fori_loop(1, 16, add, zsend[l, z_me])
        zfin[l, z_me] = (total * (1.0 / 512.0)).astype(BF16).astype(F32)
        each(1, 16, lambda j: z_back(l, j).start())

    def spread_plane(l):
        each(1, 16, lambda j: z_back(l, j).wait_recv())
        ag[l, core, plane_me] = zfin[l, :14].reshape(CHUNK, 128).astype(BF16)
        each(1, 16, lambda j: plane_back(l, j).start())
        core_back(l, 0).start()

    def forward(l):
        def pass_on(j):
            plane_back(l, j).wait_recv()
            core_back(l, j).start()

        each(1, 16, pass_on)

    def out_copy(l, h):
        return pltpu.make_async_copy(ag.at[l, h], wg.at[l, h], osem.at[l, h])

    on = maskv[...]
    g1 = jnp.where((on > 0) & (pre[1].astype(F32) > 0), cot[...].astype(F32), 0.0)
    stage(1, g1)
    pl.semaphore_wait(barrier, 8 + 1 + 30)
    for copy in side_copies(1):
        copy.start()
    place(0, 0, g1.reshape(64, 8, 128))
    x1 = jnp.where(on > 0, jnp.maximum(pre[0].astype(F32), 0.0), 0.0)
    xt[1] = x1.T.astype(BF16)
    x0 = jnp.where(on > 0, feat[...].astype(F32), 0.0)
    xt[0] = x0.T.astype(BF16)
    pg[:, 27 * 128 :] = jnp.zeros((512, 128), BF16)
    for copy in w_copies:
        copy.wait()
    for copy in side_copies(1):
        copy.wait_recv()
    rims(1)
    patches()
    d1 = input_grads(1)
    g0 = jnp.where((maskv[...] > 0) & (pre[0].astype(F32) > 0), d1, 0.0).astype(BF16).astype(F32)
    stage(0, g0)
    for copy in side_copies(0):
        copy.start()
    place(0, 0, g0.reshape(64, 8, 128))
    kernel_grads(1)
    core_copy(1).start()
    for copy in side_copies(0):
        copy.wait_recv()
    rims(0)
    patches()
    sum_halves(1)
    kernel_grads(0)
    core_copy(0).start()
    d0 = input_grads(0)
    gin[...] = jnp.where(maskv[...] > 0, d0, 0.0).astype(BF16)
    sum_halves(0)
    sum_plane(1)
    sum_z(1)
    sum_plane(0)
    spread_plane(1)
    sum_z(0)
    forward(1)
    spread_plane(0)
    each(0, 16, lambda j: core_back(1, j).wait_recv())
    for h in (0, 1):
        out_copy(1, h).start()
    forward(0)
    each(0, 16, lambda j: core_back(0, j).wait_recv())
    for h in (0, 1):
        out_copy(0, h).start()

    for l in (1, 0):
        for copy in side_copies(l):
            copy.wait_send()
        core_copy(l).wait_send()
        core_back(l, 0).wait_send()

        def sent(j):
            plane_copy(l, j).wait_send()
            z_copy(l, j).wait_send()
            z_back(l, j).wait_send()
            plane_back(l, j).wait_send()
            core_back(l, j).wait_send()

        each(1, 16, sent)
        for h in (0, 1):
            out_copy(l, h).wait()


def on_device(features, pre_acts, cotangent, weights, voxel_mask, neighbours):
    vmem = pl.BlockSpec(memory_space=pltpu.VMEM)
    anywhere = pl.BlockSpec(memory_space=pl.ANY)
    dma = pltpu.SemaphoreType.DMA
    gin, wg = pl.pallas_call(
        kernel,
        out_shape=(
            jax.ShapeDtypeStruct((512, 128), BF16),
            jax.ShapeDtypeStruct((2, 2, 16, CHUNK, 128), BF16),
        ),
        in_specs=[vmem, vmem, vmem, vmem, pl.BlockSpec(memory_space=pltpu.SMEM), anywhere],
        out_specs=(vmem, anywhere),
        scratch_shapes=[
            pltpu.VMEM((2, 27, 128, 128), BF16),
            pltpu.VMEM((512, 128), F32),
            pltpu.VMEM((3, 10, 10, 8, 128), F32),
            pltpu.VMEM((512, 28 * 128), BF16),
            pltpu.VMEM((2, 128, 512), BF16),
            pltpu.VMEM((2, 4, 64, 128), BF16),
            pltpu.VMEM((2, 4, 16, 128), BF16),
            pltpu.VMEM((2, 4, 64, 128), BF16),
            pltpu.VMEM((2, 4, 16, 128), BF16),
            pltpu.VMEM((2, 2, 16 * CHUNK, 128), F32),
            pltpu.VMEM((2, 16 * CHUNK, 128), F32),
            pltpu.VMEM((2, CHUNK, 128), F32),
            pltpu.VMEM((2, 16, CHUNK, 128), BF16),
            pltpu.VMEM((2, 15, CHUNK, 128), BF16),
            pltpu.VMEM((2, 16, 8, 128), F32),
            pltpu.VMEM((2, 15, 8, 128), F32),
            pltpu.VMEM((2, 16, 8, 128), F32),
            pltpu.VMEM((2, 2, 16, CHUNK, 128), BF16),
            dma((2,)), dma((2, 2)), dma((2, 8)), dma((2, 8)), dma((2,)), dma((2,)),
            dma((2, 15)), dma((2, 15)), dma((2, 15)), dma((2, 15)), dma((2, 15)), dma((2, 15)),
            dma((2, 15)), dma((2, 15)), dma((2, 16)), dma((2, 16)),
        ],
        compiler_params=pltpu.CompilerParams(
            collective_id=0, has_side_effects=True, vmem_limit_bytes=48 * 1024 * 1024
        ),
        cost_estimate=pl.CostEstimate(flops=2_000_000_000, bytes_accessed=5_000_000, transcendentals=0),
    )(
        features.reshape(512, 128),
        pre_acts.reshape(2, 512, 128),
        cotangent.reshape(512, 128),
        voxel_mask.reshape(1, 512),
        neighbours.reshape(1, 27),
        weights,
    )
    halves = wg.reshape(2, 2, 28, 64, 128)[:, :, :27]
    return gin.reshape(1, 1, 1, 8, 8, 8, 128), jnp.swapaxes(halves, 1, 2).reshape(2, 27, 128, 128)


def solution(mesh):
    in_specs = (
        P("gx", "gy", None, None, None, None, None),
        P(None, "gx", "gy", None, None, None, None, None),
        P("gx", "gy", None, None, None, None, None),
        P(),
        P("gx", "gy", None, None),
        P("gx", "gy", None, None),
    )
    out_specs = (P("gx", "gy", None, None, None, None, None), P())
    return jax.shard_map(
        on_device, mesh=mesh, in_specs=in_specs, out_specs=out_specs, check_vma=False
    )
```

time: 787 us -> 89.7 us (0.11)
  waiting for transfers between devices: 531 us -> 0 us
  local copies, waits for them, and re-layouts: 97.3 us -> 7.7 us
  Pallas kernels: 0 us -> 81.1 us
  between operations: 65.1 us -> 0.66 us
  starting transfers between devices: 40.1 us -> 0 us
  other arithmetic: 38.8 us -> 0 us
  matrix products: 11.6 us -> 0 us
    psum x1 -> x0, waiting for transfers between devices: 520 us -> none  [on_device(): summed = lax.psum(kernel_sums, ('gx', 'gy'))]
    pallas_call x0 -> x1, Pallas kernels: none -> 81.1 us  [on_device(): pl.pallas_call(kernel, out_shape=(jax.ShapeDtypeStruct((512, 128), BF16),...]
    reshape x54 -> x0, local copies, waits for them, and re-layouts: 46 us -> none  [patch_matrix(): windows.append(padded[:, 1 + sign * a:9 + sign * a, 1 + sign * b:9 + sign...]
    ppermute x12 -> x0, starting transfers between devices: 40.1 us -> none  [the longest x6 23.2 us: extended(): lax.ppermute(lax.slice_in_dim(block, block.shape[dim] - width, None, axis...]
    unnamed x216 -> x13, local copies, waits for them, and re-layouts: 32.5 us -> 6.22 us
    select_n x89 -> x0, other arithmetic: 25.9 us -> none  [the longest x86 24 us: assemble(): z_parts.append(jnp.take(rim_part, lookup[:, k], axis=0))]
    slice x33 -> x0, local copies, waits for them, and re-layouts: 13.1 us -> none  [the longest x22 8.82 us: assemble(): rim_part = source[:, rim_slice(a), rim_slice(b), rim_slice(c)]]
    dot_general x4 -> x0, matrix products: 11.6 us -> none  [the longest x2 6.73 us: weight_terms(): lax.dot_general(patches, flat_grad, (((0,), (0,)), ((), ())), preferred_e...]
  transfers between devices with their start and end apart: 13 -> 0, of which waited for: 3 -> 0; matrix products, arithmetic and copies ran while one was open for 2% -> 0% of each run, Pallas kernels for 0% -> 0%
where the time goes in v1:
time: 89.7 us; the launch traced here: 89.5 us
  Pallas kernels  81.1 us (90%)
  local copies, waits for them, and re-layouts  7.7 us (9%)
    pallas_call x1, Pallas kernels, on_device(): pl.pallas_call(kernel, out_shape=(jax.ShapeDtypeStruct((512, 128), BF16),...  81.1 us
    unnamed x13, local copies, waits for them, and re-layouts  6.22 us

profile of v1, /device:TPU:1, one launch (start us, length us, event | category | flops | bytes accessed | tf_op | source)
XLA Modules:
  0.0 89.5 jit_solution(2342707177781789179)
XLA Ops:
  0.6 0.0 copy-start
  0.6 1.5 %copy-done = bf16[2,27,128,128]{3,2,1,0:T(8,128)(2,1)S(1)} copy-done((bf16[2,27,128,128]{3,2,1,0:T(8,128)(2,1)S(1)}, bf16[2,27,128,128]{3,2,1,0:T(8,128)(2,1)}, u32[]{:S(2)}) %copy-start) | copy-done | bytes 1769496
  2.1 0.0 copy-start.1
  2.1 0.9 %copy-done.1 = bf16[2,1,1,1,8,8,8,128]{7,6,5,4,3,2,1,0:T(8,128)(2,1)S(1)} copy-done((bf16[2,1,1,1,8,8,8,128]{7,6,5,4,3,2,1,0:T(8,128)(2,1)S(1)}, bf16[2,1,1,1,8,8,8,128]{7,6,5,4,3,2,1,0:T(8,128)(2,1)}, u32[]{:S(2)}) %copy-start.1) | copy-done | bytes 262168
  3.1 0.0 copy-start.2
  3.1 0.9 %copy-done.2 = bf16[1,1,1,8,8,8,128]{6,5,4,3,2,1,0:T(8,128)(2,1)S(1)} copy-done((bf16[1,1,1,8,8,8,128]{6,5,4,3,2,1,0:T(8,128)(2,1)S(1)}, bf16[1,1,1,8,8,8,128]{6,5,4,3,2,1,0:T(8,128)(2,1)}, u32[]{:S(2)}) %copy-start.2) | copy-done | bytes 131096
  4.0 0.0 copy-start.3
  4.0 0.9 %copy-done.3 = bf16[1,1,1,8,8,8,128]{6,5,4,3,2,1,0:T(8,128)(2,1)S(1)} copy-done((bf16[1,1,1,8,8,8,128]{6,5,4,3,2,1,0:T(8,128)(2,1)S(1)}, bf16[1,1,1,8,8,8,128]{6,5,4,3,2,1,0:T(8,128)(2,1)}, u32[]{:S(2)}) %copy-start.3) | copy-done | bytes 131096
  4.9 0.0 copy-start.4
  4.9 0.7 copy-done.4
  5.6 0.0 copy-start.5
  5.6 0.7 copy-done.5
  6.2 81.1 %shard_map.77 = (bf16[512,128]{1,0:T(8,128)(2,1)S(1)}, bf16[2,2,16,112,128]{4,3,2,1,0:T(8,128)(2,1)S(1)}) custom-call(bf16[512,128]{1,0:T(8,128)(2,1)S(1)} %bitcast.13, bf16[2,512,128]{2,1,0:T(8,128)(2,1)S(1)} %bitcast.12, bf16[512,128]{1,0:T(8,128)(2,1)S(1)} %bitcast.14, s32[1,512]{1,0:T(1,128)S(1)} %bitcast.15, s32[1,27]{1,0:T(1,128)S(1)} %bitcast.16, ...), custom_call_target="tpu_custom_call" | custom-call | flops 2000000000 | bytes 5000000 | tf_op jit(solution)/shard_map/pallas_call | solution.py:307
  87.3 0.1 slice_bitcast_fusion
  87.5 1.3 %copy.8 = bf16[2,27,2,64,128]{4,3,2,1,0:T(8,128)(2,1)} copy(bf16[2,27,2,64,128]{4,3,1,2,0:T(8,128)(2,1)S(1)} %slice_bitcast_fusion) | data formatting | bytes 3538944 | tf_op jit(solution)/shard_map/transpose | solution.py:351
  88.8 0.7 copy.10
Async XLA Ops:
  0.6 1.5 %copy-start = (bf16[2,27,128,128]{3,2,1,0:T(8,128)(2,1)S(1)}, bf16[2,27,128,128]{3,2,1,0:T(8,128)(2,1)}, u32[]{:S(2)}) copy-start(bf16[2,27,128,128]{3,2,1,0:T(8,128)(2,1)} %w_hbm.1) | copy-start | bytes 5308420
  2.1 0.9 %copy-start.1 = (bf16[2,1,1,1,8,8,8,128]{7,6,5,4,3,2,1,0:T(8,128)(2,1)S(1)}, bf16[2,1,1,1,8,8,8,128]{7,6,5,4,3,2,1,0:T(8,128)(2,1)}, u32[]{:S(2)}) copy-start(bf16[2,1,1,1,8,8,8,128]{7,6,5,4,3,2,1,0:T(8,128)(2,1)} %param.7) | copy-start | bytes 786436
  3.1 0.9 %copy-start.2 = (bf16[1,1,1,8,8,8,128]{6,5,4,3,2,1,0:T(8,128)(2,1)S(1)}, bf16[1,1,1,8,8,8,128]{6,5,4,3,2,1,0:T(8,128)(2,1)}, u32[]{:S(2)}) copy-start(bf16[1,1,1,8,8,8,128]{6,5,4,3,2,1,0:T(8,128)(2,1)} %param.6) | copy-start | bytes 393220
  4.0 0.9 %copy-start.3 = (bf16[1,1,1,8,8,8,128]{6,5,4,3,2,1,0:T(8,128)(2,1)S(1)}, bf16[1,1,1,8,8,8,128]{6,5,4,3,2,1,0:T(8,128)(2,1)}, u32[]{:S(2)}) copy-start(bf16[1,1,1,8,8,8,128]{6,5,4,3,2,1,0:T(8,128)(2,1)} %param.8) | copy-start | bytes 393220
  4.9 0.7 copy-start.4
  5.6 0.7 copy-start.5

commit v2 on v1

v2 whole, which is shorter than its diff:
```python
import jax
import jax.numpy as jnp
from jax import lax
from jax.experimental import pallas as pl
from jax.experimental.pallas import tpu as pltpu
from jax.sharding import PartitionSpec as P

F32 = jnp.float32
BF16 = jnp.bfloat16
MESH = pl.DeviceIdType.MESH
SIDES = [(a, b) for a in (-1, 0, 1) for b in (-1, 0, 1) if (a, b) != (0, 0)]
CHUNK = 112


def kernel(
    feat_any, pre_any, cot_any, mask_any, nbr_any, w_any, gin, wg,
    feat, pre, cot, mask, nbr, wv, maskv, pad, pg, rowsT, gface, gcorner, rface, rcorner,
    s, crecv, hsum, psend, precv, zsend, zrecv, zfin, ag,
    isem, wsem, osem, hss, hrs, css, crs, pss, prs, zss, zrs, zas, zar, pas, par, cas, car,
):
    gx, gy = lax.axis_index("gx"), lax.axis_index("gy")
    z_hi, x = gx // 4, gx % 4
    y, z_lo, core = gy // 8, (gy // 2) % 4, gy % 2
    other = 1 - core
    plane_me = x * 4 + y
    z_me = z_hi * 4 + z_lo

    def plane_device(i):
        return {"gx": z_hi * 4 + i // 4, "gy": (i % 4) * 8 + z_lo * 2 + core}

    def z_device(i):
        return {"gx": (i // 4) * 4 + x, "gy": y * 8 + (i % 4) * 2 + core}

    core_device = {"gx": gx, "gy": gy + 1 - 2 * core}

    def side_device(a, b):
        return {"gx": (gx + a + 16) % 16, "gy": (gy + b + 32) % 32}

    inputs = [
        pltpu.make_async_copy(src, dst, isem.at[n])
        for n, (src, dst) in enumerate(
            ((mask_any, mask), (nbr_any, nbr), (cot_any, cot), (pre_any, pre), (feat_any, feat))
        )
    ]
    for copy in inputs:
        copy.start()

    barrier = pltpu.get_barrier_semaphore()
    for a, b in SIDES:
        pl.semaphore_signal(barrier, inc=1, device_id=side_device(a, b), device_id_type=MESH)
    pl.semaphore_signal(barrier, inc=1, device_id=core_device, device_id_type=MESH)

    def greet(j, carry):
        pl.semaphore_signal(barrier, inc=1, device_id=plane_device((plane_me + j) % 16), device_id_type=MESH)
        pl.semaphore_signal(barrier, inc=1, device_id=z_device((z_me + j) % 16), device_id_type=MESH)
        return carry

    lax.fori_loop(1, 16, greet, 0)
    w_copies = [pltpu.make_async_copy(w_any.at[l], wv.at[l], wsem.at[l]) for l in (1, 0)]
    for copy in w_copies:
        copy.start()

    for copy in inputs:
        copy.wait()
    rows = lax.broadcasted_iota(jnp.int32, (128, 128), 0)
    cols = lax.broadcasted_iota(jnp.int32, (128, 128), 1)
    ones = jnp.ones((128, 128), BF16)
    for r in range(4):
        line = (mask[:, r * 128 : (r + 1) * 128] > 0).astype(F32)
        spread = jnp.where(rows == cols, jnp.broadcast_to(line, (128, 128)), 0.0).astype(BF16)
        maskv[r * 128 : (r + 1) * 128] = jnp.dot(spread, ones, preferred_element_type=F32)

    def flag(a, b, c):
        return jnp.where(nbr[0, (a + 1) * 9 + (b + 1) * 3 + c + 1] >= 0, 1.0, 0.0)

    level = lax.broadcasted_iota(jnp.int32, (1, 8, 128), 1)

    def place(f, a, b, tile):
        low, mid, high = flag(a, b, -1), flag(a, b, 0), flag(a, b, 1)
        nx, ny = (1 if a else 8), (1 if b else 8)
        x0, y0 = {-1: 0, 0: 1, 1: 9}[a], {-1: 0, 0: 1, 1: 9}[b]
        shape = (nx, ny, 8, 128)
        below = pltpu.roll(tile, 1, 1) * jnp.where(level == 0, low, mid)
        above = pltpu.roll(tile, 7, 1) * jnp.where(level == 7, high, mid)
        pad[f, 0, x0 : x0 + nx, y0 : y0 + ny] = below.reshape(shape)
        pad[f, 1, x0 : x0 + nx, y0 : y0 + ny] = (tile * mid).reshape(shape)
        pad[f, 2, x0 : x0 + nx, y0 : y0 + ny] = above.reshape(shape)

    def side_copies(h):
        copies = []
        for n, (a, b) in enumerate(SIDES):
            m = SIDES.index((-a, -b))
            if a and b:
                i, j = (a + 1) + (b + 1) // 2, (1 - a) + (1 - b) // 2
                src, dst = gcorner.at[h, i], rcorner.at[h, j]
            else:
                i = (a + 1) // 2 if a else 2 + (b + 1) // 2
                j = (1 - a) // 2 if a else 2 + (1 - b) // 2
                src, dst = gface.at[h, i], rface.at[h, j]
            copies.append(
                pltpu.make_async_remote_copy(
                    src_ref=src, dst_ref=dst, send_sem=hss.at[h, n], recv_sem=hrs.at[h, m],
                    device_id=side_device(a, b), device_id_type=MESH,
                )
            )
        return copies

    def stage(h, v):
        v4 = v.reshape(8, 8, 8, 128)
        for i, e in ((0, 0), (1, 7)):
            gface[h, i] = v4[e].reshape(64, 128).astype(BF16)
            gface[h, 2 + i] = v4[:, e].reshape(64, 128).astype(BF16)
            for j, f in ((0, 0), (1, 7)):
                cell = v4[e, f]
                gcorner[h, 2 * i + j] = jnp.concatenate([cell, cell], axis=0).astype(BF16)

    def rims(h, f):
        for copy in side_copies(h):
            copy.wait_recv()
        for a, b in SIDES:
            if a and b:
                cell = rcorner[h, (a + 1) + (b + 1) // 2].astype(F32)[:8]
                place(f, a, b, cell.reshape(1, 8, 128))
            else:
                i = (a + 1) // 2 if a else 2 + (b + 1) // 2
                place(f, a, b, rface[h, i].astype(F32).reshape(8, 8, 128))

    def patches(f, sign):
        for k in range(27):
            a, b, c = (sign * v for v in (k // 9 - 1, (k // 3) % 3 - 1, k % 3 - 1))
            window = pad[f, 1 + c, 1 + a : 9 + a, 1 + b : 9 + b]
            pg[f, :, k * 128 : (k + 1) * 128] = window.reshape(512, 128).astype(BF16)

    def input_grads(l):
        kernels = jnp.concatenate([wv[l, k] for k in range(27)], axis=1)
        return lax.dot_general(
            pg[0, :, : 27 * 128], kernels, (((1,), (1,)), ((), ())), preferred_element_type=F32
        )

    def kernel_grads(l):
        f = 1 - l
        for m in range(14):
            both = jnp.dot(
                rowsT[f], pg[f, :, m * 256 : (m + 1) * 256], preferred_element_type=F32
            )
            for q in (0, 1):
                block = both[:, q * 128 : (q + 1) * 128]
                block = block.T if l == 0 else block
                for h in (0, 1):
                    at = m * 128 + q * 64
                    s[l, h, at : at + 64] = block[h * 64 : (h + 1) * 64]

    def part(i):
        return pl.ds(pl.multiple_of(i * CHUNK, CHUNK), CHUNK)

    def core_copy(l):
        return pltpu.make_async_remote_copy(
            src_ref=s.at[l, other], dst_ref=crecv.at[l], send_sem=css.at[l], recv_sem=crs.at[l],
            device_id=core_device, device_id_type=MESH,
        )

    def plane_copy(l, j):
        peer = (plane_me + j) % 16
        return pltpu.make_async_remote_copy(
            src_ref=psend.at[l, peer], dst_ref=precv.at[l, j - 1],
            send_sem=pss.at[l, j - 1], recv_sem=prs.at[l, j - 1],
            device_id=plane_device(peer), device_id_type=MESH,
        )

    def z_copy(l, j):
        peer = (z_me + j) % 16
        return pltpu.make_async_remote_copy(
            src_ref=zsend.at[l, peer], dst_ref=zrecv.at[l, j - 1],
            send_sem=zss.at[l, j - 1], recv_sem=zrs.at[l, j - 1],
            device_id=z_device(peer), device_id_type=MESH,
        )

    def z_back(l, j):
        return pltpu.make_async_remote_copy(
            src_ref=zfin.at[l, z_me], dst_ref=zfin.at[l, z_me],
            send_sem=zas.at[l, j - 1], recv_sem=zar.at[l, j - 1],
            device_id=z_device((z_me + j) % 16), device_id_type=MESH,
        )

    def plane_back(l, j):
        return pltpu.make_async_remote_copy(
            src_ref=ag.at[l, core, part(plane_me)], dst_ref=ag.at[l, core, part(plane_me)],
            send_sem=pas.at[l, j - 1], recv_sem=par.at[l, j - 1],
            device_id=plane_device((plane_me + j) % 16), device_id_type=MESH,
        )

    def core_back(l, j):
        owner = (plane_me + 16 - j) % 16
        return pltpu.make_async_remote_copy(
            src_ref=ag.at[l, core, part(owner)], dst_ref=ag.at[l, core, part(owner)],
            send_sem=cas.at[l, j], recv_sem=car.at[l, j],
            device_id=core_device, device_id_type=MESH,
        )

    def each(first, last, act):
        def step(j, carry):
            act(j)
            return carry

        lax.fori_loop(first, last, step, 0)

    def sum_halves(l):
        core_copy(l).wait_recv()

        def chunk(j):
            i = (plane_me + j) % 16
            total = s[l, core, part(i)] + crecv[l, part(i)]
            psend[l, i] = total.astype(BF16)
            plane_copy(l, j).start()

        each(1, 16, chunk)
        hsum[l] = s[l, core, part(plane_me)] + crecv[l, part(plane_me)]

    def sum_plane(l):
        def add(j, total):
            plane_copy(l, j).wait_recv()
            return total + precv[l, j - 1].astype(F32)

        total = lax.fori_loop(1, 16, add, hsum[l])
        zsend[l, :14] = total.reshape(14, 8, 128)
        zsend[l, 14:] = jnp.zeros((2, 8, 128), F32)
        each(1, 16, lambda j: z_copy(l, j).start())

    def sum_z(l):
        def add(j, total):
            z_copy(l, j).wait_recv()
            return total + zrecv[l, j - 1]

        total = lax.fori_loop(1, 16, add, zsend[l, z_me])
        zfin[l, z_me] = (total * (1.0 / 512.0)).astype(BF16).astype(F32)
        each(1, 16, lambda j: z_back(l, j).start())

    def spread_plane(l):
        each(1, 16, lambda j: z_back(l, j).wait_recv())
        ag[l, core, part(plane_me)] = zfin[l, :14].reshape(CHUNK, 128).astype(BF16)
        each(1, 16, lambda j: plane_back(l, j).start())
        core_back(l, 0).start()

    def forward(l):
        def pass_on(j):
            plane_back(l, j).wait_recv()
            core_back(l, j).start()

        each(1, 16, pass_on)

    def out_copy(l, h):
        return pltpu.make_async_copy(ag.at[l, h, : 27 * 64], wg.at[l, h], osem.at[l, h])

    on = maskv[...] > 0
    g1 = jnp.where(on & (pre[1].astype(F32) > 0), cot[...].astype(F32), 0.0)
    stage(0, g1)
    x0 = jnp.where(on, feat[...].astype(F32), 0.0)
    stage(1, x0)
    pl.semaphore_wait(barrier, 8 + 1 + 30)
    for h in (0, 1):
        for copy in side_copies(h):
            copy.start()
    place(0, 0, 0, g1.reshape(64, 8, 128))
    place(1, 0, 0, x0.reshape(64, 8, 128))
    x1 = jnp.where(on, jnp.maximum(pre[0].astype(F32), 0.0), 0.0)
    rowsT[0] = x1.T.astype(BF16)
    for f in (0, 1):
        pg[f, :, 27 * 128 :] = jnp.zeros((512, 128), BF16)
    for copy in w_copies:
        copy.wait()

    rims(0, 0)
    patches(0, -1)
    kernel_grads(1)
    core_copy(1).start()
    d1 = input_grads(1)
    g0 = jnp.where((maskv[...] > 0) & (pre[0].astype(F32) > 0), d1, 0.0).astype(BF16).astype(F32)
    stage(2, g0)
    for copy in side_copies(2):
        copy.start()
    rowsT[1] = g0.T.astype(BF16)
    place(0, 0, 0, g0.reshape(64, 8, 128))
    rims(1, 1)
    patches(1, 1)
    sum_halves(1)
    kernel_grads(0)
    core_copy(0).start()
    sum_halves(0)
    rims(2, 0)
    patches(0, -1)
    d0 = input_grads(0)
    gin[...] = jnp.where(maskv[...] > 0, d0, 0.0).astype(BF16)

    sum_plane(1)
    sum_plane(0)
    sum_z(1)
    sum_z(0)
    spread_plane(1)
    spread_plane(0)
    forward(1)
    forward(0)
    for l in (1, 0):
        each(0, 16, lambda j: core_back(l, j).wait_recv())
        for h in (0, 1):
            out_copy(l, h).start()

    for h in (0, 1, 2):
        for copy in side_copies(h):
            copy.wait_send()
    for l in (1, 0):
        core_copy(l).wait_send()
        core_back(l, 0).wait_send()

        def sent(j):
            plane_copy(l, j).wait_send()
            z_copy(l, j).wait_send()
            z_back(l, j).wait_send()
            plane_back(l, j).wait_send()
            core_back(l, j).wait_send()

        each(1, 16, sent)
        for h in (0, 1):
            out_copy(l, h).wait()


def on_device(features, pre_acts, cotangent, weights, voxel_mask, neighbours):
    vmem = pl.BlockSpec(memory_space=pltpu.VMEM)
    anywhere = pl.BlockSpec(memory_space=pl.ANY)
    dma = pltpu.SemaphoreType.DMA
    gin, wg = pl.pallas_call(
        kernel,
        out_shape=(
            jax.ShapeDtypeStruct((512, 128), BF16),
            jax.ShapeDtypeStruct((2, 2, 27 * 64, 128), BF16),
        ),
        in_specs=[anywhere] * 6,
        out_specs=(vmem, anywhere),
        scratch_shapes=[
            pltpu.VMEM((512, 128), BF16),
            pltpu.VMEM((2, 512, 128), BF16),
            pltpu.VMEM((512, 128), BF16),
            pltpu.VMEM((1, 512), jnp.int32),
            pltpu.SMEM((1, 27), jnp.int32),
            pltpu.VMEM((2, 27, 128, 128), BF16),
            pltpu.VMEM((512, 128), F32),
            pltpu.VMEM((2, 3, 10, 10, 8, 128), F32),
            pltpu.VMEM((2, 512, 28 * 128), BF16),
            pltpu.VMEM((2, 128, 512), BF16),
            pltpu.VMEM((3, 4, 64, 128), BF16),
            pltpu.VMEM((3, 4, 16, 128), BF16),
            pltpu.VMEM((3, 4, 64, 128), BF16),
            pltpu.VMEM((3, 4, 16, 128), BF16),
            pltpu.VMEM((2, 2, 16 * CHUNK, 128), F32),
            pltpu.VMEM((2, 16 * CHUNK, 128), F32),
            pltpu.VMEM((2, CHUNK, 128), F32),
            pltpu.VMEM((2, 16, CHUNK, 128), BF16),
            pltpu.VMEM((2, 15, CHUNK, 128), BF16),
            pltpu.VMEM((2, 16, 8, 128), F32),
            pltpu.VMEM((2, 15, 8, 128), F32),
            pltpu.VMEM((2, 16, 8, 128), F32),
            pltpu.VMEM((2, 2, 16 * CHUNK, 128), BF16),
            dma((5,)), dma((2,)), dma((2, 2)), dma((3, 8)), dma((3, 8)), dma((2,)), dma((2,)),
            dma((2, 15)), dma((2, 15)), dma((2, 15)), dma((2, 15)), dma((2, 15)), dma((2, 15)),
            dma((2, 15)), dma((2, 15)), dma((2, 16)), dma((2, 16)),
        ],
        compiler_params=pltpu.CompilerParams(
            collective_id=0, has_side_effects=True, vmem_limit_bytes=64 * 1024 * 1024
        ),
        cost_estimate=pl.CostEstimate(flops=2_000_000_000, bytes_accessed=5_000_000, transcendentals=0),
    )(
        features.reshape(512, 128),
        pre_acts.reshape(2, 512, 128),
        cotangent.reshape(512, 128),
        voxel_mask.reshape(1, 512),
        neighbours.reshape(1, 27),
        weights,
    )
    halves = wg.reshape(2, 2, 27, 64, 128)
    return gin.reshape(1, 1, 1, 8, 8, 8, 128), jnp.swapaxes(halves, 1, 2).reshape(2, 27, 128, 128)


def solution(mesh):
    in_specs = (
        P("gx", "gy", None, None, None, None, None),
        P(None, "gx", "gy", None, None, None, None, None),
        P("gx", "gy", None, None, None, None, None),
        P(),
        P("gx", "gy", None, None),
        P("gx", "gy", None, None),
    )
    out_specs = (P("gx", "gy", None, None, None, None, None), P())
    return jax.shard_map(
        on_device, mesh=mesh, in_specs=in_specs, out_specs=out_specs, check_vma=False
    )
```

time: 89.7 us -> 79.3 us (0.88)
  Pallas kernels: 81.1 us -> 74.9 us
  local copies, waits for them, and re-layouts: 7.7 us -> 3.58 us
    pallas_call x1, Pallas kernels: 81.1 us -> 74.9 us  [on_device(): pl.pallas_call(kernel, out_shape=(jax.ShapeDtypeStruct((512, 128), BF16),...]
    unnamed x13 -> x3, local copies, waits for them, and re-layouts: 6.22 us -> 0.66 us
    transpose x2 -> x1, local copies, waits for them, and re-layouts: 1.48 us -> 2.92 us  [on_device(): jnp.swapaxes(halves, 1, 2).reshape(2, 27, 128, 128)]
where the time goes in v2:
time: 79.3 us; the launch traced here: 79.2 us
  Pallas kernels  74.9 us (94%)
  local copies, waits for them, and re-layouts  3.58 us (5%)
    pallas_call x1, Pallas kernels, on_device(): pl.pallas_call(kernel, out_shape=(jax.ShapeDtypeStruct((512, 128), BF16),...  74.9 us
    transpose x1, local copies, waits for them, and re-layouts, on_device(): jnp.swapaxes(halves, 1, 2).reshape(2, 27, 128, 128)  2.92 us

profile of v2, /device:TPU:1, one launch (start us, length us, event | category | flops | bytes accessed | tf_op | source)
XLA Modules:
  0.0 79.2 jit_solution(9221368661649501814)
XLA Ops:
  0.6 74.9 %shard_map.77 = (bf16[512,128]{1,0:T(8,128)(2,1)}, bf16[2,2,1728,128]{3,2,1,0:T(8,128)(2,1)}) custom-call(bf16[512,128]{1,0:T(8,128)(2,1)} %bitcast.14, bf16[2,512,128]{2,1,0:T(8,128)(2,1)} %bitcast.13, bf16[512,128]{1,0:T(8,128)(2,1)} %bitcast.15, s32[1,512]{1,0:T(1,128)} %bitcast.16, s32[1,27]{1,0:T(1,128)} %bitcast.17, bf16[2,27,128,128]{3,2,1,0:T(8,128)(2,1)} %w_any.1), custom_call_target="tpu_custom_call" | custom-call | flops 2000000000 | bytes 5000000 | tf_op jit(solution)/shard_map/pallas_call | solution.py:330
  75.6 0.0 copy-start
  75.6 2.9 %copy.8 = bf16[2,27,2,64,128]{4,3,2,1,0:T(8,128)(2,1)} copy(bf16[2,27,2,64,128]{4,3,1,2,0:T(8,128)(2,1)} %bitcast.11) | data formatting | bytes 3538944 | tf_op jit(solution)/shard_map/transpose | solution.py:379
  78.5 0.0 copy-done
  78.5 0.7 copy.10
Async XLA Ops:
  75.6 2.9 %copy-start = (bf16[512,128]{1,0:T(8,128)(2,1)S(1)}, bf16[512,128]{1,0:T(8,128)(2,1)}, u32[]{:S(2)}) copy-start(bf16[512,128]{1,0:T(8,128)(2,1)} %get-tuple-element.4) | copy-start | bytes 393220

commit v3 on v2

v3 whole, which is shorter than its diff:
```python
import jax
import jax.numpy as jnp
from jax import lax
from jax.experimental import pallas as pl
from jax.experimental.pallas import tpu as pltpu
from jax.sharding import PartitionSpec as P

F32 = jnp.float32
BF16 = jnp.bfloat16
MESH = pl.DeviceIdType.MESH
SIDES = [(a, b) for a in (-1, 0, 1) for b in (-1, 0, 1) if (a, b) != (0, 0)]
BATCHES = ((1, 0, 64, 0), (1, 1024, 48, 8), (0, 0, 64, 0), (0, 1024, 48, 8))
HALF = 27 * 64


def kernel(
    feat_any, pre_any, cot_any, mask_any, nbr_any, w_any, gin, wg,
    feat, pre, cot, mask, nbr, wv, maskv, pad, pg, rowsT, gface, gcorner, rface, rcorner,
    s, crecv, psend, precv, zsend, zrecv, zfin, ag,
    isem, wsem, osem, hss, hrs, css, crs, pss, prs, zss, zrs, zas, zar, pas, par, cas, car,
):
    gx, gy = lax.axis_index("gx"), lax.axis_index("gy")
    z_hi, x = gx // 4, gx % 4
    y, z_lo, core = gy // 8, (gy // 2) % 4, gy % 2
    other = 1 - core
    plane_me = x * 4 + y
    z_me = z_hi * 4 + z_lo

    def plane_device(i):
        return {"gx": z_hi * 4 + i // 4, "gy": (i % 4) * 8 + z_lo * 2 + core}

    def z_device(i):
        return {"gx": (i // 4) * 4 + x, "gy": y * 8 + (i % 4) * 2 + core}

    core_device = {"gx": gx, "gy": gy + 1 - 2 * core}

    def side_device(a, b):
        return {"gx": (gx + a + 16) % 16, "gy": (gy + b + 32) % 32}

    def plane_shift(i):
        v = i + i // 10
        return (2 + v // 4) % 4, (2 + v % 4) % 4

    def plane_to(i):
        dx, dy = plane_shift(i)
        return ((x + dx) % 4) * 4 + (y + dy) % 4

    def plane_from(i):
        dx, dy = plane_shift(i)
        return ((x + 4 - dx) % 4) * 4 + (y + 4 - dy) % 4

    def z_far(i):
        return 8 + (i // 2) - (i % 2) * (2 * (i // 2) + 1)

    inputs = [
        pltpu.make_async_copy(src, dst, isem.at[n])
        for n, (src, dst) in enumerate(
            ((mask_any, mask), (nbr_any, nbr), (cot_any, cot), (pre_any, pre), (feat_any, feat))
        )
    ]
    for copy in inputs:
        copy.start()

    barrier = pltpu.get_barrier_semaphore()
    for a, b in SIDES:
        pl.semaphore_signal(barrier, inc=1, device_id=side_device(a, b), device_id_type=MESH)
    pl.semaphore_signal(barrier, inc=1, device_id=core_device, device_id_type=MESH)

    def greet(j, carry):
        pl.semaphore_signal(barrier, inc=1, device_id=plane_device((plane_me + j) % 16), device_id_type=MESH)
        pl.semaphore_signal(barrier, inc=1, device_id=z_device((z_me + j) % 16), device_id_type=MESH)
        return carry

    lax.fori_loop(1, 16, greet, 0)
    w_copies = [pltpu.make_async_copy(w_any.at[l], wv.at[l], wsem.at[l]) for l in (1, 0)]
    for copy in w_copies:
        copy.start()

    for copy in inputs:
        copy.wait()
    rows = lax.broadcasted_iota(jnp.int32, (128, 128), 0)
    cols = lax.broadcasted_iota(jnp.int32, (128, 128), 1)
    ones = jnp.ones((128, 128), BF16)
    for r in range(4):
        line = (mask[:, r * 128 : (r + 1) * 128] > 0).astype(F32)
        spread = jnp.where(rows == cols, jnp.broadcast_to(line, (128, 128)), 0.0).astype(BF16)
        maskv[r * 128 : (r + 1) * 128] = jnp.dot(spread, ones, preferred_element_type=F32)

    def flag(a, b, c):
        return jnp.where(nbr[0, (a + 1) * 9 + (b + 1) * 3 + c + 1] >= 0, 1.0, 0.0)

    level = lax.broadcasted_iota(jnp.int32, (1, 8, 128), 1)

    def place(f, a, b, tile):
        low, mid, high = flag(a, b, -1), flag(a, b, 0), flag(a, b, 1)
        nx, ny = (1 if a else 8), (1 if b else 8)
        x0, y0 = {-1: 0, 0: 1, 1: 9}[a], {-1: 0, 0: 1, 1: 9}[b]
        shape = (nx, ny, 8, 128)
        below = pltpu.roll(tile, 1, 1) * jnp.where(level == 0, low, mid)
        above = pltpu.roll(tile, 7, 1) * jnp.where(level == 7, high, mid)
        pad[f, 0, x0 : x0 + nx, y0 : y0 + ny] = below.reshape(shape)
        pad[f, 1, x0 : x0 + nx, y0 : y0 + ny] = (tile * mid).reshape(shape)
        pad[f, 2, x0 : x0 + nx, y0 : y0 + ny] = above.reshape(shape)

    def side_copies(group):
        copies = []
        for a, b in SIDES:
            if (group in (0, 3)) != bool(a and b):
                continue
            if a and b:
                i, j = (a + 1) + (b + 1) // 2, (1 - a) + (1 - b) // 2
                src, dst = gcorner.at[group // 3, i], rcorner.at[group // 3, j]
            else:
                i = (a + 1) // 2 if a else 2 + (b + 1) // 2
                j = (1 - a) // 2 if a else 2 + (1 - b) // 2
                face = {1: 0, 2: 1, 4: 2}[group]
                src, dst = gface.at[face, i], rface.at[face, j]
            copies.append(
                pltpu.make_async_remote_copy(
                    src_ref=src, dst_ref=dst, send_sem=hss.at[group, i], recv_sem=hrs.at[group, j],
                    device_id=side_device(a, b), device_id_type=MESH,
                )
            )
        return copies

    def stage_corners(n, first, second):
        for i in (0, 1):
            for j in (0, 1):
                cells = [v.reshape(8, 8, 8, 128)[7 * i, 7 * j] for v in (first, second)]
                gcorner[n, 2 * i + j] = jnp.concatenate(cells, axis=0).astype(BF16)

    def stage_faces(n, v):
        v4 = v.reshape(8, 8, 8, 128)
        for i in (0, 1):
            gface[n, i] = v4[7 * i].reshape(64, 128).astype(BF16)
            gface[n, 2 + i] = v4[:, 7 * i].reshape(64, 128).astype(BF16)

    def rims(f, corners, row, face):
        for a, b in SIDES:
            if a and b:
                cell = rcorner[corners, (a + 1) + (b + 1) // 2].astype(F32)[row : row + 8]
                place(f, a, b, cell.reshape(1, 8, 128))
            else:
                i = (a + 1) // 2 if a else 2 + (b + 1) // 2
                place(f, a, b, rface[face, i].astype(F32).reshape(8, 8, 128))

    def patches(f, sign):
        for k in range(27):
            a, b, c = (sign * v for v in (k // 9 - 1, (k // 3) % 3 - 1, k % 3 - 1))
            window = pad[f, 1 + c, 1 + a : 9 + a, 1 + b : 9 + b]
            pg[f, :, k * 128 : (k + 1) * 128] = window.reshape(512, 128).astype(BF16)

    def input_grads(l):
        kernels = jnp.concatenate([wv[l, k] for k in range(27)], axis=1)
        return lax.dot_general(
            pg[0, :, : 27 * 128], kernels, (((1,), (1,)), ((), ())), preferred_element_type=F32
        )

    def kernel_grads(l, first, last):
        f = 1 - l
        for m in range(first, last):
            both = jnp.dot(
                rowsT[f], pg[f, :, m * 256 : (m + 1) * 256], preferred_element_type=F32
            )
            for q in (0, 1):
                block = both[:, q * 128 : (q + 1) * 128]
                block = block.T if l == 0 else block
                for h in (0, 1):
                    at = m * 128 + q * 64
                    s[l, h, at : at + 64] = block[h * 64 : (h + 1) * 64]

    def part(b, i):
        _, base, chunk, _ = BATCHES[b]
        return pl.ds(pl.multiple_of(base + i * chunk, 16), chunk)

    def core_copy(b):
        l, base, chunk, _ = BATCHES[b]
        rows = pl.ds(base, 16 * chunk)
        return pltpu.make_async_remote_copy(
            src_ref=s.at[l, other, rows], dst_ref=crecv.at[l, rows],
            send_sem=css.at[b], recv_sem=crs.at[b],
            device_id=core_device, device_id_type=MESH,
        )

    def plane_copy(b, i):
        l, _, chunk, _ = BATCHES[b]
        peer = plane_to(i)
        return pltpu.make_async_remote_copy(
            src_ref=psend.at[l, part(b, peer)], dst_ref=precv.at[b, i, pl.ds(0, chunk)],
            send_sem=pss.at[b, i], recv_sem=prs.at[b, i],
            device_id=plane_device(peer), device_id_type=MESH,
        )

    def z_copy(b, o, sender):
        return pltpu.make_async_remote_copy(
            src_ref=zsend.at[b, o], dst_ref=zrecv.at[b, sender],
            send_sem=zss.at[b, o], recv_sem=zrs.at[b, sender],
            device_id=z_device(BATCHES[b][3] + o), device_id_type=MESH,
        )

    def z_back(b, i, o):
        return pltpu.make_async_remote_copy(
            src_ref=zfin.at[b, o], dst_ref=zfin.at[b, o],
            send_sem=zas.at[b, i], recv_sem=zar.at[b, o],
            device_id=z_device((z_me + z_far(i)) % 16), device_id_type=MESH,
        )

    def plane_back(b, i):
        l = BATCHES[b][0]
        rows = part(b, plane_me)
        return pltpu.make_async_remote_copy(
            src_ref=ag.at[l, core, rows], dst_ref=ag.at[l, core, rows],
            send_sem=pas.at[b, i], recv_sem=par.at[b, i],
            device_id=plane_device(plane_to(i)), device_id_type=MESH,
        )

    def core_back(b, n, owner):
        l = BATCHES[b][0]
        rows = part(b, owner)
        return pltpu.make_async_remote_copy(
            src_ref=ag.at[l, core, rows], dst_ref=ag.at[l, core, rows],
            send_sem=cas.at[b, n], recv_sem=car.at[b, n],
            device_id=core_device, device_id_type=MESH,
        )

    def each(first, last, act):
        def step(j, carry):
            act(j)
            return carry

        lax.fori_loop(first, last, step, 0)

    def sum_halves(b):
        l = BATCHES[b][0]
        core_copy(b).wait_recv()

        def chunk(i):
            rows = part(b, plane_to(i))
            psend[l, rows] = (s[l, core, rows] + crecv[l, rows]).astype(BF16)
            plane_copy(b, i).start()

        each(0, 15, chunk)

    def owned(b):
        return z_me - BATCHES[b][3]

    def owns(b):
        return (owned(b) >= 0) & (owned(b) < BATCHES[b][2] // 8)

    def sum_plane(b):
        l, _, chunk, _ = BATCHES[b]

        def add(t, total):
            i = 14 - t
            plane_copy(b, i).wait_recv()
            return total + precv[b, i, pl.ds(0, chunk)].astype(F32)

        rows = part(b, plane_me)
        total = lax.fori_loop(0, 15, add, s[l, core, rows] + crecv[l, rows])
        zsend[b, : chunk // 8] = total.reshape(chunk // 8, 8, 128)

        def send(o):
            @pl.when(owned(b) != o)
            def _():
                z_copy(b, o, z_me).start()

        each(0, chunk // 8, send)

    def sum_z(b):
        @pl.when(owns(b))
        def _():
            o = owned(b)

            def add(t, total):
                sender = (z_me + z_far(14 - t)) % 16
                z_copy(b, o, sender).wait_recv()
                return total + zrecv[b, sender]

            total = lax.fori_loop(0, 15, add, zsend[b, o])
            zfin[b, o] = (total * (1.0 / 512.0)).astype(BF16).astype(F32)
            each(0, 15, lambda i: z_back(b, i, o).start())

    def spread_plane(b):
        l, _, chunk, _ = BATCHES[b]

        def arrive(o):
            @pl.when(owned(b) != o)
            def _():
                z_back(b, 0, o).wait_recv()

        each(0, chunk // 8, arrive)
        ag[l, core, part(b, plane_me)] = zfin[b, : chunk // 8].reshape(chunk, 128).astype(BF16)
        each(0, 15, lambda i: plane_back(b, i).start())
        core_back(b, 15, plane_me).start()

    def out_copy(b, h, n):
        l, base, chunk, _ = BATCHES[b]
        rows = pl.ds(base, min(16 * chunk, HALF - base))
        return pltpu.make_async_copy(ag.at[l, h, rows], wg.at[l, h, rows], osem.at[b, n])

    def forward(b):
        def pass_on(t):
            i = 14 - t
            plane_back(b, i).wait_recv()
            core_back(b, i, plane_from(i)).start()

        each(0, 15, pass_on)
        out_copy(b, core, 0).start()

    def finish(b):
        each(0, 16, lambda n: core_back(b, n, plane_me).wait_recv())
        out_copy(b, other, 1).start()

    on = maskv[...] > 0
    g1 = jnp.where(on & (pre[1].astype(F32) > 0), cot[...].astype(F32), 0.0)
    x0 = jnp.where(on, feat[...].astype(F32), 0.0)
    stage_corners(0, g1, x0)
    stage_faces(0, g1)
    pl.semaphore_wait(barrier, 8 + 1 + 30)
    for group in (0, 1):
        for copy in side_copies(group):
            copy.start()
    stage_faces(1, x0)
    for copy in side_copies(2):
        copy.start()
    place(0, 0, 0, g1.reshape(64, 8, 128))
    place(1, 0, 0, x0.reshape(64, 8, 128))
    x1 = jnp.where(on, jnp.maximum(pre[0].astype(F32), 0.0), 0.0)
    rowsT[0] = x1.T.astype(BF16)
    for f in (0, 1):
        pg[f, :, 27 * 128 :] = jnp.zeros((512, 128), BF16)

    for group in (0, 1):
        for copy in side_copies(group):
            copy.wait_recv()
    rims(0, 0, 0, 0)
    patches(0, -1)
    kernel_grads(1, 0, 8)
    core_copy(0).start()
    kernel_grads(1, 8, 14)
    core_copy(1).start()
    for copy in w_copies:
        copy.wait()
    d1 = input_grads(1)
    g0 = jnp.where((maskv[...] > 0) & (pre[0].astype(F32) > 0), d1, 0.0).astype(BF16).astype(F32)
    stage_corners(1, g0, g0)
    stage_faces(2, g0)
    for group in (3, 4):
        for copy in side_copies(group):
            copy.start()
    rowsT[1] = g0.T.astype(BF16)
    place(0, 0, 0, g0.reshape(64, 8, 128))
    sum_halves(0)
    sum_halves(1)
    for copy in side_copies(2):
        copy.wait_recv()
    rims(1, 0, 8, 1)
    patches(1, 1)
    kernel_grads(0, 0, 8)
    core_copy(2).start()
    kernel_grads(0, 8, 14)
    core_copy(3).start()
    sum_halves(2)
    sum_halves(3)
    sum_plane(0)
    sum_plane(1)
    for group in (3, 4):
        for copy in side_copies(group):
            copy.wait_recv()
    rims(0, 1, 0, 2)
    patches(0, -1)
    d0 = input_grads(0)
    gin[...] = jnp.where(maskv[...] > 0, d0, 0.0).astype(BF16)

    sum_plane(2)
    sum_plane(3)
    for act in (sum_z, spread_plane, forward, finish):
        for b in range(4):
            act(b)

    for group in range(5):
        for copy in side_copies(group):
            copy.wait_send()
    for b in range(4):
        core_copy(b).wait_send()
        core_back(b, 15, plane_me).wait_send()

        def sent(i):
            plane_copy(b, i).wait_send()
            plane_back(b, i).wait_send()
            core_back(b, i, plane_me).wait_send()

        each(0, 15, sent)

        def sent_z(o):
            @pl.when(owned(b) != o)
            def _():
                z_copy(b, o, z_me).wait_send()

        each(0, BATCHES[b][2] // 8, sent_z)

        @pl.when(owns(b))
        def _():
            each(0, 15, lambda i: z_back(b, i, owned(b)).wait_send())

        out_copy(b, core, 0).wait()
        out_copy(b, other, 1).wait()


def on_device(features, pre_acts, cotangent, weights, voxel_mask, neighbours):
    vmem = pl.BlockSpec(memory_space=pltpu.VMEM)
    anywhere = pl.BlockSpec(memory_space=pl.ANY)
    dma = pltpu.SemaphoreType.DMA
    gin, wg = pl.pallas_call(
        kernel,
        out_shape=(
            jax.ShapeDtypeStruct((512, 128), BF16),
            jax.ShapeDtypeStruct((2, 2, HALF, 128), BF16),
        ),
        in_specs=[anywhere] * 6,
        out_specs=(vmem, anywhere),
        scratch_shapes=[
            pltpu.VMEM((512, 128), BF16),
            pltpu.VMEM((2, 512, 128), BF16),
            pltpu.VMEM((512, 128), BF16),
            pltpu.VMEM((1, 512), jnp.int32),
            pltpu.SMEM((1, 27), jnp.int32),
            pltpu.VMEM((2, 27, 128, 128), BF16),
            pltpu.VMEM((512, 128), F32),
            pltpu.VMEM((2, 3, 10, 10, 8, 128), F32),
            pltpu.VMEM((2, 512, 28 * 128), BF16),
            pltpu.VMEM((2, 128, 512), BF16),
            pltpu.VMEM((3, 4, 64, 128), BF16),
            pltpu.VMEM((2, 4, 16, 128), BF16),
            pltpu.VMEM((3, 4, 64, 128), BF16),
            pltpu.VMEM((2, 4, 16, 128), BF16),
            pltpu.VMEM((2, 2, 28 * 64, 128), F32),
            pltpu.VMEM((2, 28 * 64, 128), F32),
            pltpu.VMEM((2, 28 * 64, 128), BF16),
            pltpu.VMEM((4, 15, 64, 128), BF16),
            pltpu.VMEM((4, 8, 8, 128), F32),
            pltpu.VMEM((4, 16, 8, 128), F32),
            pltpu.VMEM((4, 8, 8, 128), F32),
            pltpu.VMEM((2, 2, 28 * 64, 128), BF16),
            dma((5,)), dma((2,)), dma((4, 2)), dma((5, 4)), dma((5, 4)), dma((4,)), dma((4,)),
            dma((4, 15)), dma((4, 15)), dma((4, 8)), dma((4, 16)), dma((4, 15)), dma((4, 8)),
            dma((4, 15)), dma((4, 15)), dma((4, 16)), dma((4, 16)),
        ],
        compiler_params=pltpu.CompilerParams(
            collective_id=0, has_side_effects=True, vmem_limit_bytes=64 * 1024 * 1024
        ),
        cost_estimate=pl.CostEstimate(flops=2_000_000_000, bytes_accessed=5_000_000, transcendentals=0),
    )(
        features.reshape(512, 128),
        pre_acts.reshape(2, 512, 128),
        cotangent.reshape(512, 128),
        voxel_mask.reshape(1, 512),
        neighbours.reshape(1, 27),
        weights,
    )
    halves = wg.reshape(2, 2, 27, 64, 128)
    return gin.reshape(1, 1, 1, 8, 8, 8, 128), jnp.swapaxes(halves, 1, 2).reshape(2, 27, 128, 128)


def solution(mesh):
    in_specs = (
        P("gx", "gy", None, None, None, None, None),
        P(None, "gx", "gy", None, None, None, None, None),
        P("gx", "gy", None, None, None, None, None),
        P(),
        P("gx", "gy", None, None),
        P("gx", "gy", None, None),
    )
    out_specs = (P("gx", "gy", None, None, None, None, None), P())
    return jax.shard_map(
        on_device, mesh=mesh, in_specs=in_specs, out_specs=out_specs, check_vma=False
    )
```

time: 79.3 us -> 74.6 us (0.941)
  Pallas kernels: 74.9 us -> 70.2 us
    pallas_call x1, Pallas kernels: 74.9 us -> 70.2 us  [on_device(): pl.pallas_call(kernel, out_shape=(jax.ShapeDtypeStruct((512, 128), BF16),...]
where the time goes in v3:
time: 74.6 us; the launch traced here: 74.5 us
  Pallas kernels  70.2 us (94%)
  local copies, waits for them, and re-layouts  3.58 us (5%)
    pallas_call x1, Pallas kernels, on_device(): pl.pallas_call(kernel, out_shape=(jax.ShapeDtypeStruct((512, 128), BF16),...  70.2 us
    transpose x1, local copies, waits for them, and re-layouts, on_device(): jnp.swapaxes(halves, 1, 2).reshape(2, 27, 128, 128)  2.92 us

profile of v3, /device:TPU:1, one launch (start us, length us, event | category | flops | bytes accessed | tf_op | source)
XLA Modules:
  0.0 74.5 jit_solution(14116364500016364538)
XLA Ops:
  0.6 70.2 %shard_map.77 = (bf16[512,128]{1,0:T(8,128)(2,1)}, bf16[2,2,1728,128]{3,2,1,0:T(8,128)(2,1)}) custom-call(bf16[512,128]{1,0:T(8,128)(2,1)} %bitcast.14, bf16[2,512,128]{2,1,0:T(8,128)(2,1)} %bitcast.13, bf16[512,128]{1,0:T(8,128)(2,1)} %bitcast.15, s32[1,512]{1,0:T(1,128)} %bitcast.16, s32[1,27]{1,0:T(1,128)} %bitcast.17, bf16[2,27,128,128]{3,2,1,0:T(8,128)(2,1)} %w_any.1), custom_call_target="tpu_custom_call" | custom-call | flops 2000000000 | bytes 5000000 | tf_op jit(solution)/shard_map/pallas_call | solution.py:414
  70.9 0.0 copy-start
  70.9 2.9 %copy.8 = bf16[2,27,2,64,128]{4,3,2,1,0:T(8,128)(2,1)} copy(bf16[2,27,2,64,128]{4,3,1,2,0:T(8,128)(2,1)} %bitcast.11) | data formatting | bytes 3538944 | tf_op jit(solution)/shard_map/transpose | solution.py:462
  73.8 0.0 copy-done
  73.8 0.7 copy.10
Async XLA Ops:
  70.9 2.9 %copy-start = (bf16[512,128]{1,0:T(8,128)(2,1)S(1)}, bf16[512,128]{1,0:T(8,128)(2,1)}, u32[]{:S(2)}) copy-start(bf16[512,128]{1,0:T(8,128)(2,1)} %get-tuple-element.4) | copy-start | bytes 393220

commit v4 on v3

--- a/solution.py
+++ b/solution.py
@@ -17,7 +17,7 @@
     feat_any, pre_any, cot_any, mask_any, nbr_any, w_any, gin, wg,
     feat, pre, cot, mask, nbr, wv, maskv, pad, pg, rowsT, gface, gcorner, rface, rcorner,
     s, crecv, psend, precv, zsend, zrecv, zfin, ag,
-    isem, wsem, osem, hss, hrs, css, crs, pss, prs, zss, zrs, zas, zar, pas, par, cas, car,
+    isem, wsem, osem, hss, hrs, css, crs, pss, prs, zss, zrs, zas, zar, pas, par, cas, car, relays,
 ):
     gx, gy = lax.axis_index("gx"), lax.axis_index("gy")
     z_hi, x = gx // 4, gx % 4
@@ -62,16 +62,28 @@
         copy.start()
 
     barrier = pltpu.get_barrier_semaphore()
+
+    def greet(sem, device):
+        pl.semaphore_signal(sem, inc=1, device_id=device, device_id_type=MESH)
+
+    def relay(step):
+        for shift in (2**step, 16 - 2**step):
+            greet(relays.at[step], z_device((z_me + shift) % 16))
+
+    def relayed(step):
+        pl.semaphore_wait(relays.at[step], 2)
+
     for a, b in SIDES:
-        pl.semaphore_signal(barrier, inc=1, device_id=side_device(a, b), device_id_type=MESH)
-    pl.semaphore_signal(barrier, inc=1, device_id=core_device, device_id_type=MESH)
-
-    def greet(j, carry):
-        pl.semaphore_signal(barrier, inc=1, device_id=plane_device((plane_me + j) % 16), device_id_type=MESH)
-        pl.semaphore_signal(barrier, inc=1, device_id=z_device((z_me + j) % 16), device_id_type=MESH)
+        greet(barrier, side_device(a, b))
+    greet(barrier, core_device)
+    for shift in (1, 15):
+        greet(barrier, z_device((z_me + shift) % 16))
+
+    def greet_plane(i, carry):
+        greet(barrier, plane_device(plane_to(i)))
         return carry
 
-    lax.fori_loop(1, 16, greet, 0)
+    lax.fori_loop(0, 15, greet_plane, 0)
     w_copies = [pltpu.make_async_copy(w_any.at[l], wv.at[l], wsem.at[l]) for l in (1, 0)]
     for copy in w_copies:
         copy.start()
@@ -296,7 +308,10 @@
     def out_copy(b, h, n):
         l, base, chunk, _ = BATCHES[b]
         rows = pl.ds(base, min(16 * chunk, HALF - base))
-        return pltpu.make_async_copy(ag.at[l, h, rows], wg.at[l, h, rows], osem.at[b, n])
+        kernels = pl.ds(base // 64, rows.size // 64)
+        return pltpu.make_async_copy(
+            ag.reshape(2, 2, 28, 64, 128).at[l, h, kernels], wg.at[l, kernels, h], osem.at[b, n]
+        )
 
     def forward(b):
         def pass_on(t):
@@ -316,13 +331,14 @@
     x0 = jnp.where(on, feat[...].astype(F32), 0.0)
     stage_corners(0, g1, x0)
     stage_faces(0, g1)
-    pl.semaphore_wait(barrier, 8 + 1 + 30)
+    pl.semaphore_wait(barrier, 8 + 1 + 2 + 15)
     for group in (0, 1):
         for copy in side_copies(group):
             copy.start()
     stage_faces(1, x0)
     for copy in side_copies(2):
         copy.start()
+    relay(0)
     place(0, 0, 0, g1.reshape(64, 8, 128))
     place(1, 0, 0, x0.reshape(64, 8, 128))
     x1 = jnp.where(on, jnp.maximum(pre[0].astype(F32), 0.0), 0.0)
@@ -339,6 +355,8 @@
     core_copy(0).start()
     kernel_grads(1, 8, 14)
     core_copy(1).start()
+    relayed(0)
+    relay(1)
     for copy in w_copies:
         copy.wait()
     d1 = input_grads(1)
@@ -352,6 +370,8 @@
     place(0, 0, 0, g0.reshape(64, 8, 128))
     sum_halves(0)
     sum_halves(1)
+    relayed(1)
+    relay(2)
     for copy in side_copies(2):
         copy.wait_recv()
     rims(1, 0, 8, 1)
@@ -362,6 +382,7 @@
     core_copy(3).start()
     sum_halves(2)
     sum_halves(3)
+    relayed(2)
     sum_plane(0)
     sum_plane(1)
     for group in (3, 4):
@@ -415,7 +436,7 @@
         kernel,
         out_shape=(
             jax.ShapeDtypeStruct((512, 128), BF16),
-            jax.ShapeDtypeStruct((2, 2, HALF, 128), BF16),
+            jax.ShapeDtypeStruct((2, 27, 2, 64, 128), BF16),
         ),
         in_specs=[anywhere] * 6,
         out_specs=(vmem, anywhere),
@@ -444,22 +465,26 @@
             pltpu.VMEM((2, 2, 28 * 64, 128), BF16),
             dma((5,)), dma((2,)), dma((4, 2)), dma((5, 4)), dma((5, 4)), dma((4,)), dma((4,)),
             dma((4, 15)), dma((4, 15)), dma((4, 8)), dma((4, 16)), dma((4, 15)), dma((4, 8)),
-            dma((4, 15)), dma((4, 15)), dma((4, 16)), dma((4, 16)),
+            dma((4, 15)), dma((4, 15)), dma((4, 16)), dma((4, 16)), pltpu.SemaphoreType.REGULAR((3,)),
         ],
         compiler_params=pltpu.CompilerParams(
-            collective_id=0, has_side_effects=True, vmem_limit_bytes=64 * 1024 * 1024
+            collective_id=0, has_side_effects=True, vmem_limit_bytes=40 * 1024 * 1024
         ),
         cost_estimate=pl.CostEstimate(flops=2_000_000_000, bytes_accessed=5_000_000, transcendentals=0),
     )(
-        features.reshape(512, 128),
-        pre_acts.reshape(2, 512, 128),
-        cotangent.reshape(512, 128),
-        voxel_mask.reshape(1, 512),
-        neighbours.reshape(1, 27),
-        weights,
+        *(
+            pltpu.with_memory_space_constraint(v, pltpu.HBM)
+            for v in (
+                features.reshape(512, 128),
+                pre_acts.reshape(2, 512, 128),
+                cotangent.reshape(512, 128),
+                voxel_mask.reshape(1, 512),
+                neighbours.reshape(1, 27),
+                weights,
+            )
+        )
     )
-    halves = wg.reshape(2, 2, 27, 64, 128)
-    return gin.reshape(1, 1, 1, 8, 8, 8, 128), jnp.swapaxes(halves, 1, 2).reshape(2, 27, 128, 128)
+    return gin.reshape(1, 1, 1, 8, 8, 8, 128), wg.reshape(2, 27, 128, 128)
 
 
 def solution(mesh):

time: 74.6 us -> 71.4 us (0.957)
  local copies, waits for them, and re-layouts: 3.58 us -> 1.86 us
  Pallas kernels: 70.2 us -> 68.8 us
    transpose x1 -> x0, local copies, waits for them, and re-layouts: 2.92 us -> none  [on_device(): jnp.swapaxes(halves, 1, 2).reshape(2, 27, 128, 128)]
    pallas_call x1, Pallas kernels: 70.2 us -> 68.8 us  [on_device(): pl.pallas_call(kernel, out_shape=(jax.ShapeDtypeStruct((512, 128), BF16),...]
    unnamed x3 -> x2, local copies, waits for them, and re-layouts: 0.66 us -> 1.86 us
where the time goes in v4:
time: 71.4 us; the launch traced here: 71.3 us
  Pallas kernels  68.8 us (96%)
  local copies, waits for them, and re-layouts  1.86 us (3%)
    pallas_call x1, Pallas kernels, on_device(): pl.pallas_call(kernel, out_shape=(jax.ShapeDtypeStruct((512, 128), BF16),...  68.8 us
    unnamed x2, local copies, waits for them, and re-layouts  1.86 us

profile of v4, /device:TPU:1, one launch (start us, length us, event | category | flops | bytes accessed | tf_op | source)
XLA Modules:
  0.0 71.3 jit_solution(3920718353434875928)
XLA Ops:
  0.6 68.8 %shard_map.77 = (bf16[512,128]{1,0:T(8,128)(2,1)S(1)}, bf16[2,27,2,64,128]{4,3,2,1,0:T(8,128)(2,1)S(1)}) custom-call(bf16[512,128]{1,0:T(8,128)(2,1)} %bitcast.10, bf16[2,512,128]{2,1,0:T(8,128)(2,1)} %bitcast.9, bf16[512,128]{1,0:T(8,128)(2,1)} %bitcast.11, s32[1,512]{1,0:T(1,128)} %bitcast.12, s32[1,27]{1,0:T(1,128)} %bitcast.13, ...), custom_call_target="tpu_custom_call" | custom-call | flops 2000000000 | bytes 5000000 | tf_op jit(solution)/shard_map/pallas_call | solution.py:435
  69.4 0.7 copy.10
  70.1 1.2 %copy.11 = bf16[2,27,128,128]{3,2,1,0:T(8,128)(2,1)} copy(bf16[2,27,128,128]{3,2,1,0:T(8,128)(2,1)S(1)} %bitcast.7) | data formatting | bytes 3538944

commit v5 on v4

--- a/solution.py
+++ b/solution.py
@@ -9,29 +9,30 @@
 BF16 = jnp.bfloat16
 MESH = pl.DeviceIdType.MESH
 SIDES = [(a, b) for a in (-1, 0, 1) for b in (-1, 0, 1) if (a, b) != (0, 0)]
-BATCHES = ((1, 0, 64, 0), (1, 1024, 48, 8), (0, 0, 64, 0), (0, 1024, 48, 8))
+BATCHES = ((1, 0, 64), (1, 1024, 48), (0, 0, 64), (0, 1024, 48))
 HALF = 27 * 64
 
 
 def kernel(
     feat_any, pre_any, cot_any, mask_any, nbr_any, w_any, gin, wg,
     feat, pre, cot, mask, nbr, wv, maskv, pad, pg, rowsT, gface, gcorner, rface, rcorner,
-    s, crecv, psend, precv, zsend, zrecv, zfin, ag,
-    isem, wsem, osem, hss, hrs, css, crs, pss, prs, zss, zrs, zas, zar, pas, par, cas, car, relays,
+    s, crecv, psend, precv, zrecv, ag,
+    isem, wsem, osem, hss, hrs, css, crs, pss, prs, zss, zrs, pas, par, cas, car, relays,
 ):
     gx, gy = lax.axis_index("gx"), lax.axis_index("gy")
     z_hi, x = gx // 4, gx % 4
     y, z_lo, core = gy // 8, (gy // 2) % 4, gy % 2
     other = 1 - core
     plane_me = x * 4 + y
-    z_me = z_hi * 4 + z_lo
-
-    def plane_device(i):
-        return {"gx": z_hi * 4 + i // 4, "gy": (i % 4) * 8 + z_lo * 2 + core}
+    member, place_z = z_lo % 2, z_hi * 2 + z_lo // 2
+
+    def plane_device(i, m):
+        return {"gx": z_hi * 4 + i // 4, "gy": (i % 4) * 8 + (z_lo - member + m) * 2 + core}
 
     def z_device(i):
-        return {"gx": (i // 4) * 4 + x, "gy": y * 8 + (i % 4) * 2 + core}
-
+        return {"gx": (i // 2) * 4 + x, "gy": y * 8 + ((i % 2) * 2 + member) * 2 + core}
+
+    partner = {"gx": gx, "gy": gy + 2 - 4 * member}
     core_device = {"gx": gx, "gy": gy + 1 - 2 * core}
 
     def side_device(a, b):
@@ -50,7 +51,7 @@
         return ((x + 4 - dx) % 4) * 4 + (y + 4 - dy) % 4
 
     def z_far(i):
-        return 8 + (i // 2) - (i % 2) * (2 * (i // 2) + 1)
+        return 4 + (i // 2) - (i % 2) * (2 * (i // 2) + 1)
 
     inputs = [
         pltpu.make_async_copy(src, dst, isem.at[n])
@@ -67,8 +68,8 @@
         pl.semaphore_signal(sem, inc=1, device_id=device, device_id_type=MESH)
 
     def relay(step):
-        for shift in (2**step, 16 - 2**step):
-            greet(relays.at[step], z_device((z_me + shift) % 16))
+        for shift in (2**step, 8 - 2**step):
+            greet(relays.at[step], z_device((place_z + shift) % 8))
 
     def relayed(step):
         pl.semaphore_wait(relays.at[step], 2)
@@ -76,11 +77,13 @@
     for a, b in SIDES:
         greet(barrier, side_device(a, b))
     greet(barrier, core_device)
-    for shift in (1, 15):
-        greet(barrier, z_device((z_me + shift) % 16))
+    greet(barrier, partner)
+    for shift in (1, 7):
+        greet(barrier, z_device((place_z + shift) % 8))
 
     def greet_plane(i, carry):
-        greet(barrier, plane_device(plane_to(i)))
+        for m in (0, 1):
+            greet(barrier, plane_device(plane_to(i), m))
         return carry
 
     lax.fori_loop(0, 15, greet_plane, 0)
@@ -182,11 +185,26 @@
                     s[l, h, at : at + 64] = block[h * 64 : (h + 1) * 64]
 
     def part(b, i):
-        _, base, chunk, _ = BATCHES[b]
+        _, base, chunk = BATCHES[b]
         return pl.ds(pl.multiple_of(base + i * chunk, 16), chunk)
 
+    def piece(b, i, m, n):
+        _, base, chunk = BATCHES[b]
+        return pl.ds(pl.multiple_of(base + i * chunk + 32 * m, 16), n)
+
+    def by_member(b, act):
+        sizes = (32, BATCHES[b][2] - 32)
+        if sizes[0] == sizes[1]:
+            act(member, *sizes)
+            return
+        for m in (0, 1):
+
+            @pl.when(member == m)
+            def _():
+                act(m, sizes[m], sizes[1 - m])
+
     def core_copy(b):
-        l, base, chunk, _ = BATCHES[b]
+        l, base, chunk = BATCHES[b]
         rows = pl.ds(base, 16 * chunk)
         return pltpu.make_async_remote_copy(
             src_ref=s.at[l, other, rows], dst_ref=crecv.at[l, rows],
@@ -194,36 +212,66 @@
             device_id=core_device, device_id_type=MESH,
         )
 
-    def plane_copy(b, i):
-        l, _, chunk, _ = BATCHES[b]
+    def plane_copy(b, i, m, n):
         peer = plane_to(i)
         return pltpu.make_async_remote_copy(
-            src_ref=psend.at[l, part(b, peer)], dst_ref=precv.at[b, i, pl.ds(0, chunk)],
-            send_sem=pss.at[b, i], recv_sem=prs.at[b, i],
-            device_id=plane_device(peer), device_id_type=MESH,
-        )
-
-    def z_copy(b, o, sender):
-        return pltpu.make_async_remote_copy(
-            src_ref=zsend.at[b, o], dst_ref=zrecv.at[b, sender],
-            send_sem=zss.at[b, o], recv_sem=zrs.at[b, sender],
-            device_id=z_device(BATCHES[b][3] + o), device_id_type=MESH,
-        )
-
-    def z_back(b, i, o):
-        return pltpu.make_async_remote_copy(
-            src_ref=zfin.at[b, o], dst_ref=zfin.at[b, o],
-            send_sem=zas.at[b, i], recv_sem=zar.at[b, o],
-            device_id=z_device((z_me + z_far(i)) % 16), device_id_type=MESH,
-        )
-
-    def plane_back(b, i):
-        l = BATCHES[b][0]
-        rows = part(b, plane_me)
-        return pltpu.make_async_remote_copy(
-            src_ref=ag.at[l, core, rows], dst_ref=ag.at[l, core, rows],
-            send_sem=pas.at[b, i], recv_sem=par.at[b, i],
-            device_id=plane_device(plane_to(i)), device_id_type=MESH,
+            src_ref=psend.at[BATCHES[b][0], piece(b, peer, m, n)],
+            dst_ref=precv.at[b, 2 * i + member, pl.ds(0, n)],
+            send_sem=pss.at[b, 2 * i + m], recv_sem=prs.at[b, 2 * i + member],
+            device_id=plane_device(peer, m), device_id_type=MESH,
+        )
+
+    def pair_copy(b, m, n):
+        return pltpu.make_async_remote_copy(
+            src_ref=psend.at[BATCHES[b][0], piece(b, plane_me, m, n)],
+            dst_ref=precv.at[b, 30, pl.ds(0, n)],
+            send_sem=pss.at[b, 30], recv_sem=prs.at[b, 30],
+            device_id=partner, device_id_type=MESH,
+        )
+
+    def plane_arrival(b, slot, n):
+        rows = precv.at[b, slot, pl.ds(0, n)]
+        return pltpu.make_async_remote_copy(
+            src_ref=rows, dst_ref=rows, send_sem=pss.at[b, slot], recv_sem=prs.at[b, slot],
+            device_id=partner, device_id_type=MESH,
+        )
+
+    def z_copy(b, i, n):
+        rows = zrecv.at[b, place_z, pl.ds(0, n)]
+        return pltpu.make_async_remote_copy(
+            src_ref=rows, dst_ref=rows, send_sem=zss.at[b, i], recv_sem=zrs.at[b, place_z],
+            device_id=z_device((place_z + z_far(i)) % 8), device_id_type=MESH,
+        )
+
+    def z_arrival(b, i, n):
+        sender = (place_z + z_far(i)) % 8
+        rows = zrecv.at[b, sender, pl.ds(0, n)]
+        return pltpu.make_async_remote_copy(
+            src_ref=rows, dst_ref=rows, send_sem=zss.at[b, i], recv_sem=zrs.at[b, sender],
+            device_id=partner, device_id_type=MESH,
+        )
+
+    def plane_back(b, i, to, m, n):
+        rows = ag.at[BATCHES[b][0], core, piece(b, plane_me, m, n)]
+        return pltpu.make_async_remote_copy(
+            src_ref=rows, dst_ref=rows,
+            send_sem=pas.at[b, 2 * i + to], recv_sem=par.at[b, 2 * i + member],
+            device_id=plane_device(plane_to(i), to), device_id_type=MESH,
+        )
+
+    def plane_return(b, i, m, n):
+        rows = ag.at[BATCHES[b][0], core, piece(b, plane_from(i), m, n)]
+        return pltpu.make_async_remote_copy(
+            src_ref=rows, dst_ref=rows,
+            send_sem=pas.at[b, 2 * i + m], recv_sem=par.at[b, 2 * i + m],
+            device_id=partner, device_id_type=MESH,
+        )
+
+    def pair_back(b, m, n):
+        rows = ag.at[BATCHES[b][0], core, piece(b, plane_me, m, n)]
+        return pltpu.make_async_remote_copy(
+            src_ref=rows, dst_ref=rows, send_sem=pas.at[b, 30], recv_sem=par.at[b, 30],
+            device_id=partner, device_id_type=MESH,
         )
 
     def core_back(b, n, owner):
@@ -243,70 +291,58 @@
         lax.fori_loop(first, last, step, 0)
 
     def sum_halves(b):
-        l = BATCHES[b][0]
+        l, _, size = BATCHES[b]
         core_copy(b).wait_recv()
 
         def chunk(i):
             rows = part(b, plane_to(i))
             psend[l, rows] = (s[l, core, rows] + crecv[l, rows]).astype(BF16)
-            plane_copy(b, i).start()
+            plane_copy(b, i, 0, 32).start()
+            plane_copy(b, i, 1, size - 32).start()
 
         each(0, 15, chunk)
-
-    def owned(b):
-        return z_me - BATCHES[b][3]
-
-    def owns(b):
-        return (owned(b) >= 0) & (owned(b) < BATCHES[b][2] // 8)
+        rows = part(b, plane_me)
+        psend[l, rows] = (s[l, core, rows] + crecv[l, rows]).astype(BF16)
+        by_member(b, lambda m, n, k: pair_copy(b, 1 - m, k).start())
 
     def sum_plane(b):
-        l, _, chunk, _ = BATCHES[b]
-
-        def add(t, total):
-            i = 14 - t
-            plane_copy(b, i).wait_recv()
-            return total + precv[b, i, pl.ds(0, chunk)].astype(F32)
-
-        rows = part(b, plane_me)
-        total = lax.fori_loop(0, 15, add, s[l, core, rows] + crecv[l, rows])
-        zsend[b, : chunk // 8] = total.reshape(chunk // 8, 8, 128)
-
-        def send(o):
-            @pl.when(owned(b) != o)
-            def _():
-                z_copy(b, o, z_me).start()
-
-        each(0, chunk // 8, send)
+        l = BATCHES[b][0]
+
+        def total_of(m, n, k):
+            def add(t, total):
+                plane_arrival(b, 30 - t, n).wait_recv()
+                return total + precv[b, 30 - t, pl.ds(0, n)].astype(F32)
+
+            rows = piece(b, plane_me, m, n)
+            total = lax.fori_loop(0, 31, add, s[l, core, rows] + crecv[l, rows])
+            zrecv[b, place_z, pl.ds(0, n)] = total.astype(BF16)
+            each(0, 7, lambda i: z_copy(b, i, n).start())
+
+        by_member(b, total_of)
 
     def sum_z(b):
-        @pl.when(owns(b))
-        def _():
-            o = owned(b)
-
-            def add(t, total):
-                sender = (z_me + z_far(14 - t)) % 16
-                z_copy(b, o, sender).wait_recv()
-                return total + zrecv[b, sender]
-
-            total = lax.fori_loop(0, 15, add, zsend[b, o])
-            zfin[b, o] = (total * (1.0 / 512.0)).astype(BF16).astype(F32)
-            each(0, 15, lambda i: z_back(b, i, o).start())
-
-    def spread_plane(b):
-        l, _, chunk, _ = BATCHES[b]
-
-        def arrive(o):
-            @pl.when(owned(b) != o)
-            def _():
-                z_back(b, 0, o).wait_recv()
-
-        each(0, chunk // 8, arrive)
-        ag[l, core, part(b, plane_me)] = zfin[b, : chunk // 8].reshape(chunk, 128).astype(BF16)
-        each(0, 15, lambda i: plane_back(b, i).start())
-        core_back(b, 15, plane_me).start()
+        l = BATCHES[b][0]
+
+        def total_of(m, n, k):
+            each(0, 7, lambda i: z_arrival(b, 6 - i, n).wait_recv())
+
+            def add(q, total):
+                return total + zrecv[b, q, pl.ds(0, n)].astype(F32)
+
+            total = lax.fori_loop(0, 8, add, jnp.zeros((n, 128), F32))
+            ag[l, core, piece(b, plane_me, m, n)] = (total * (1.0 / 512.0)).astype(BF16)
+
+            def send(i):
+                plane_back(b, i, 0, m, n).start()
+                plane_back(b, i, 1, m, n).start()
+
+            each(0, 15, send)
+            pair_back(b, m, n).start()
+
+        by_member(b, total_of)
 
     def out_copy(b, h, n):
-        l, base, chunk, _ = BATCHES[b]
+        l, base, chunk = BATCHES[b]
         rows = pl.ds(base, min(16 * chunk, HALF - base))
         kernels = pl.ds(base // 64, rows.size // 64)
         return pltpu.make_async_copy(
@@ -316,9 +352,12 @@
     def forward(b):
         def pass_on(t):
             i = 14 - t
-            plane_back(b, i).wait_recv()
+            plane_return(b, i, 0, 32).wait_recv()
+            plane_return(b, i, 1, BATCHES[b][2] - 32).wait_recv()
             core_back(b, i, plane_from(i)).start()
 
+        by_member(b, lambda m, n, k: pair_back(b, 1 - m, k).wait_recv())
+        core_back(b, 15, plane_me).start()
         each(0, 15, pass_on)
         out_copy(b, core, 0).start()
 
@@ -331,7 +370,7 @@
     x0 = jnp.where(on, feat[...].astype(F32), 0.0)
     stage_corners(0, g1, x0)
     stage_faces(0, g1)
-    pl.semaphore_wait(barrier, 8 + 1 + 2 + 15)
+    pl.semaphore_wait(barrier, 8 + 1 + 1 + 2 + 30)
     for group in (0, 1):
         for copy in side_copies(group):
             copy.start()
@@ -370,8 +409,6 @@
     place(0, 0, 0, g0.reshape(64, 8, 128))
     sum_halves(0)
     sum_halves(1)
-    relayed(1)
-    relay(2)
     for copy in side_copies(2):
         copy.wait_recv()
     rims(1, 0, 8, 1)
@@ -382,7 +419,7 @@
     core_copy(3).start()
     sum_halves(2)
     sum_halves(3)
-    relayed(2)
+    relayed(1)
     sum_plane(0)
     sum_plane(1)
     for group in (3, 4):
@@ -395,7 +432,7 @@
 
     sum_plane(2)
     sum_plane(3)
-    for act in (sum_z, spread_plane, forward, finish):
+    for act in (sum_z, forward, finish):
         for b in range(4):
             act(b)
 
@@ -407,23 +444,24 @@
         core_back(b, 15, plane_me).wait_send()
 
         def sent(i):
-            plane_copy(b, i).wait_send()
-            plane_back(b, i).wait_send()
+            plane_copy(b, i, 0, 32).wait_send()
+            plane_copy(b, i, 1, BATCHES[b][2] - 32).wait_send()
             core_back(b, i, plane_me).wait_send()
 
         each(0, 15, sent)
 
-        def sent_z(o):
-            @pl.when(owned(b) != o)
-            def _():
-                z_copy(b, o, z_me).wait_send()
-
-        each(0, BATCHES[b][2] // 8, sent_z)
-
-        @pl.when(owns(b))
-        def _():
-            each(0, 15, lambda i: z_back(b, i, owned(b)).wait_send())
-
+        def sent_own(m, n, k):
+            pair_copy(b, 1 - m, k).wait_send()
+            pair_back(b, m, n).wait_send()
+            each(0, 7, lambda i: z_copy(b, i, n).wait_send())
+
+            def sent_back(i):
+                plane_back(b, i, 0, m, n).wait_send()
+                plane_back(b, i, 1, m, n).wait_send()
+
+            each(0, 15, sent_back)
+
+        by_member(b, sent_own)
         out_copy(b, core, 0).wait()
         out_copy(b, other, 1).wait()
 
@@ -458,14 +496,12 @@
             pltpu.VMEM((2, 2, 28 * 64, 128), F32),
             pltpu.VMEM((2, 28 * 64, 128), F32),
             pltpu.VMEM((2, 28 * 64, 128), BF16),
-            pltpu.VMEM((4, 15, 64, 128), BF16),
-            pltpu.VMEM((4, 8, 8, 128), F32),
-            pltpu.VMEM((4, 16, 8, 128), F32),
-            pltpu.VMEM((4, 8, 8, 128), F32),
+            pltpu.VMEM((4, 31, 32, 128), BF16),
+            pltpu.VMEM((4, 8, 32, 128), BF16),
             pltpu.VMEM((2, 2, 28 * 64, 128), BF16),
             dma((5,)), dma((2,)), dma((4, 2)), dma((5, 4)), dma((5, 4)), dma((4,)), dma((4,)),
-            dma((4, 15)), dma((4, 15)), dma((4, 8)), dma((4, 16)), dma((4, 15)), dma((4, 8)),
-            dma((4, 15)), dma((4, 15)), dma((4, 16)), dma((4, 16)), pltpu.SemaphoreType.REGULAR((3,)),
+            dma((4, 31)), dma((4, 31)), dma((4, 7)), dma((4, 8)),
+            dma((4, 31)), dma((4, 31)), dma((4, 16)), dma((4, 16)), pltpu.SemaphoreType.REGULAR((2,)),
         ],
         compiler_params=pltpu.CompilerParams(
             collective_id=0, has_side_effects=True, vmem_limit_bytes=40 * 1024 * 1024

time: 71.4 us -> 74.5 us (1.043)
  the two profiles are of different devices: /device:TPU:1 before, /device:TPU:65 now
where the time goes in v5:
time: 74.5 us; the launch traced here: 74.4 us
  Pallas kernels  71.9 us (97%)
  local copies, waits for them, and re-layouts  1.86 us (2%)
    pallas_call x1, Pallas kernels, on_device(): pl.pallas_call(kernel, out_shape=(jax.ShapeDtypeStruct((512, 128), BF16),...  71.9 us
    unnamed x2, local copies, waits for them, and re-layouts  1.86 us

profile of v5, /device:TPU:65, one launch (start us, length us, event | category | flops | bytes accessed | tf_op | source)
XLA Modules:
  0.0 74.4 jit_solution(10988959945134076731)
XLA Ops:
  0.6 71.9 %shard_map.77 = (bf16[512,128]{1,0:T(8,128)(2,1)S(1)}, bf16[2,27,2,64,128]{4,3,2,1,0:T(8,128)(2,1)S(1)}) custom-call(bf16[512,128]{1,0:T(8,128)(2,1)} %bitcast.10, bf16[2,512,128]{2,1,0:T(8,128)(2,1)} %bitcast.9, bf16[512,128]{1,0:T(8,128)(2,1)} %bitcast.11, s32[1,512]{1,0:T(1,128)} %bitcast.12, s32[1,27]{1,0:T(1,128)} %bitcast.13, ...), custom_call_target="tpu_custom_call" | custom-call | flops 2000000000 | bytes 5000000 | tf_op jit(solution)/shard_map/pallas_call | solution.py:473
  72.5 0.7 copy.10
  73.2 1.2 %copy.11 = bf16[2,27,128,128]{3,2,1,0:T(8,128)(2,1)} copy(bf16[2,27,128,128]{3,2,1,0:T(8,128)(2,1)S(1)} %bitcast.7) | data formatting | bytes 3538944

commit v6 on v4

--- a/solution.py
+++ b/solution.py
@@ -9,7 +9,7 @@
 BF16 = jnp.bfloat16
 MESH = pl.DeviceIdType.MESH
 SIDES = [(a, b) for a in (-1, 0, 1) for b in (-1, 0, 1) if (a, b) != (0, 0)]
-BATCHES = ((1, 0, 64, 0), (1, 1024, 48, 8), (0, 0, 64, 0), (0, 1024, 48, 8))
+BATCHES = ((1, 0, 64, 0), (1, 1024, 48, 2), (0, 0, 64, 1), (0, 1024, 48, 3))
 HALF = 27 * 64
 
 
@@ -199,21 +199,38 @@
         peer = plane_to(i)
         return pltpu.make_async_remote_copy(
             src_ref=psend.at[l, part(b, peer)], dst_ref=precv.at[b, i, pl.ds(0, chunk)],
-            send_sem=pss.at[b, i], recv_sem=prs.at[b, i],
+            send_sem=pss.at[b], recv_sem=prs.at[b],
             device_id=plane_device(peer), device_id_type=MESH,
         )
 
-    def z_copy(b, o, sender):
-        return pltpu.make_async_remote_copy(
-            src_ref=zsend.at[b, o], dst_ref=zrecv.at[b, sender],
-            send_sem=zss.at[b, o], recv_sem=zrs.at[b, sender],
-            device_id=z_device(BATCHES[b][3] + o), device_id_type=MESH,
-        )
+    def z_copy(b, o):
+        owner = BATCHES[b][3] + 4 * o
+        return pltpu.make_async_remote_copy(
+            src_ref=zsend.at[b, o], dst_ref=zrecv.at[b, (owner + 15 - z_me) % 16],
+            send_sem=zss.at[b, o], recv_sem=zrs.at[b],
+            device_id=z_device(owner), device_id_type=MESH,
+        )
+
+    def bytes_of(ref, send_sem, recv_sem):
+        return pltpu.make_async_remote_copy(
+            src_ref=ref, dst_ref=ref, send_sem=send_sem, recv_sem=recv_sem,
+            device_id=core_device, device_id_type=MESH,
+        )
+
+    def plane_all(b):
+        return bytes_of(precv.at[b, :, pl.ds(0, BATCHES[b][2])], pss.at[b], prs.at[b])
+
+    def z_all(b):
+        return bytes_of(zrecv.at[b], zas.at[b], zrs.at[b])
+
+    def back_all(b, count, send_sem, recv_sem):
+        l, base, chunk, _ = BATCHES[b]
+        return bytes_of(ag.at[l, core, pl.ds(base, count * chunk)], send_sem, recv_sem)
 
     def z_back(b, i, o):
         return pltpu.make_async_remote_copy(
             src_ref=zfin.at[b, o], dst_ref=zfin.at[b, o],
-            send_sem=zas.at[b, i], recv_sem=zar.at[b, o],
+            send_sem=zas.at[b], recv_sem=zar.at[b, o],
             device_id=z_device((z_me + z_far(i)) % 16), device_id_type=MESH,
         )
 
@@ -222,16 +239,16 @@
         rows = part(b, plane_me)
         return pltpu.make_async_remote_copy(
             src_ref=ag.at[l, core, rows], dst_ref=ag.at[l, core, rows],
-            send_sem=pas.at[b, i], recv_sem=par.at[b, i],
+            send_sem=pas.at[b], recv_sem=par.at[b, i],
             device_id=plane_device(plane_to(i)), device_id_type=MESH,
         )
 
-    def core_back(b, n, owner):
+    def core_back(b, owner):
         l = BATCHES[b][0]
         rows = part(b, owner)
         return pltpu.make_async_remote_copy(
             src_ref=ag.at[l, core, rows], dst_ref=ag.at[l, core, rows],
-            send_sem=cas.at[b, n], recv_sem=car.at[b, n],
+            send_sem=cas.at[b], recv_sem=car.at[b],
             device_id=core_device, device_id_type=MESH,
         )
 
@@ -253,57 +270,56 @@
 
         each(0, 15, chunk)
 
-    def owned(b):
-        return z_me - BATCHES[b][3]
+    def mine(b, o):
+        return (z_lo == BATCHES[b][3]) & (z_hi == o)
 
     def owns(b):
-        return (owned(b) >= 0) & (owned(b) < BATCHES[b][2] // 8)
+        return (z_lo == BATCHES[b][3]) & (z_hi < BATCHES[b][2] // 16)
 
     def sum_plane(b):
         l, _, chunk, _ = BATCHES[b]
 
-        def add(t, total):
-            i = 14 - t
-            plane_copy(b, i).wait_recv()
+        def add(i, total):
             return total + precv[b, i, pl.ds(0, chunk)].astype(F32)
 
+        plane_all(b).wait_recv()
         rows = part(b, plane_me)
         total = lax.fori_loop(0, 15, add, s[l, core, rows] + crecv[l, rows])
-        zsend[b, : chunk // 8] = total.reshape(chunk // 8, 8, 128)
+        zsend[b, : chunk // 16] = total.reshape(chunk // 16, 16, 128).astype(BF16)
 
         def send(o):
-            @pl.when(owned(b) != o)
+            @pl.when(jnp.logical_not(mine(b, o)))
             def _():
-                z_copy(b, o, z_me).start()
-
-        each(0, chunk // 8, send)
+                z_copy(b, o).start()
+
+        each(0, chunk // 16, send)
 
     def sum_z(b):
         @pl.when(owns(b))
         def _():
-            o = owned(b)
-
-            def add(t, total):
-                sender = (z_me + z_far(14 - t)) % 16
-                z_copy(b, o, sender).wait_recv()
-                return total + zrecv[b, sender]
-
-            total = lax.fori_loop(0, 15, add, zsend[b, o])
-            zfin[b, o] = (total * (1.0 / 512.0)).astype(BF16).astype(F32)
+            o = z_hi
+
+            def add(i, total):
+                return total + zrecv[b, i].astype(F32)
+
+            z_all(b).wait_recv()
+
+            total = lax.fori_loop(0, 15, add, zsend[b, o].astype(F32))
+            zfin[b, o] = (total * (1.0 / 512.0)).astype(BF16)
             each(0, 15, lambda i: z_back(b, i, o).start())
 
     def spread_plane(b):
         l, _, chunk, _ = BATCHES[b]
 
         def arrive(o):
-            @pl.when(owned(b) != o)
+            @pl.when(jnp.logical_not(mine(b, o)))
             def _():
                 z_back(b, 0, o).wait_recv()
 
-        each(0, chunk // 8, arrive)
-        ag[l, core, part(b, plane_me)] = zfin[b, : chunk // 8].reshape(chunk, 128).astype(BF16)
+        each(0, chunk // 16, arrive)
+        ag[l, core, part(b, plane_me)] = zfin[b, : chunk // 16].reshape(chunk, 128)
         each(0, 15, lambda i: plane_back(b, i).start())
-        core_back(b, 15, plane_me).start()
+        core_back(b, plane_me).start()
 
     def out_copy(b, h, n):
         l, base, chunk, _ = BATCHES[b]
@@ -317,13 +333,13 @@
         def pass_on(t):
             i = 14 - t
             plane_back(b, i).wait_recv()
-            core_back(b, i, plane_from(i)).start()
+            core_back(b, plane_from(i)).start()
 
         each(0, 15, pass_on)
         out_copy(b, core, 0).start()
 
     def finish(b):
-        each(0, 16, lambda n: core_back(b, n, plane_me).wait_recv())
+        back_all(b, 16, cas.at[b], car.at[b]).wait_recv()
         out_copy(b, other, 1).start()
 
     on = maskv[...] > 0
@@ -367,15 +383,14 @@
         for copy in side_copies(group):
             copy.start()
     rowsT[1] = g0.T.astype(BF16)
-    place(0, 0, 0, g0.reshape(64, 8, 128))
+    for copy in side_copies(2):
+        copy.wait_recv()
+    rims(1, 0, 8, 1)
+    patches(1, 1)
     sum_halves(0)
     sum_halves(1)
     relayed(1)
     relay(2)
-    for copy in side_copies(2):
-        copy.wait_recv()
-    rims(1, 0, 8, 1)
-    patches(1, 1)
     kernel_grads(0, 0, 8)
     core_copy(2).start()
     kernel_grads(0, 8, 14)
@@ -388,6 +403,7 @@
     for group in (3, 4):
         for copy in side_copies(group):
             copy.wait_recv()
+    place(0, 0, 0, g0.reshape(64, 8, 128))
     rims(0, 1, 0, 2)
     patches(0, -1)
     d0 = input_grads(0)
@@ -395,35 +411,42 @@
 
     sum_plane(2)
     sum_plane(3)
-    for act in (sum_z, spread_plane, forward, finish):
-        for b in range(4):
-            act(b)
-
     for group in range(5):
         for copy in side_copies(group):
             copy.wait_send()
     for b in range(4):
         core_copy(b).wait_send()
-        core_back(b, 15, plane_me).wait_send()
-
-        def sent(i):
-            plane_copy(b, i).wait_send()
-            plane_back(b, i).wait_send()
-            core_back(b, i, plane_me).wait_send()
-
-        each(0, 15, sent)
+        plane_all(b).wait_send()
+    for b in range(4):
+        sum_z(b)
+    for b in range(4):
 
         def sent_z(o):
-            @pl.when(owned(b) != o)
+            @pl.when(jnp.logical_not(mine(b, o)))
             def _():
-                z_copy(b, o, z_me).wait_send()
-
-        each(0, BATCHES[b][2] // 8, sent_z)
+                z_copy(b, o).wait_send()
+
+        each(0, BATCHES[b][2] // 16, sent_z)
+    for b in range(4):
+        spread_plane(b)
+    for b in range(4):
 
         @pl.when(owns(b))
         def _():
-            each(0, 15, lambda i: z_back(b, i, owned(b)).wait_send())
-
+            z_all(b).wait_send()
+
+    forward(0)
+    forward(1)
+    finish(0)
+    forward(2)
+    finish(1)
+    forward(3)
+    finish(2)
+    finish(3)
+
+    for b in range(4):
+        back_all(b, 15, pas.at[b], car.at[b]).wait_send()
+        back_all(b, 16, cas.at[b], car.at[b]).wait_send()
         out_copy(b, core, 0).wait()
         out_copy(b, other, 1).wait()
 
@@ -459,13 +482,13 @@
             pltpu.VMEM((2, 28 * 64, 128), F32),
             pltpu.VMEM((2, 28 * 64, 128), BF16),
             pltpu.VMEM((4, 15, 64, 128), BF16),
-            pltpu.VMEM((4, 8, 8, 128), F32),
-            pltpu.VMEM((4, 16, 8, 128), F32),
-            pltpu.VMEM((4, 8, 8, 128), F32),
+            pltpu.VMEM((4, 4, 16, 128), BF16),
+            pltpu.VMEM((4, 15, 16, 128), BF16),
+            pltpu.VMEM((4, 4, 16, 128), BF16),
             pltpu.VMEM((2, 2, 28 * 64, 128), BF16),
             dma((5,)), dma((2,)), dma((4, 2)), dma((5, 4)), dma((5, 4)), dma((4,)), dma((4,)),
-            dma((4, 15)), dma((4, 15)), dma((4, 8)), dma((4, 16)), dma((4, 15)), dma((4, 8)),
-            dma((4, 15)), dma((4, 15)), dma((4, 16)), dma((4, 16)), pltpu.SemaphoreType.REGULAR((3,)),
+            dma((4,)), dma((4,)), dma((4, 4)), dma((4,)), dma((4,)), dma((4, 4)),
+            dma((4,)), dma((4, 15)), dma((4,)), dma((4,)), pltpu.SemaphoreType.REGULAR((3,)),
         ],
         compiler_params=pltpu.CompilerParams(
             collective_id=0, has_side_effects=True, vmem_limit_bytes=40 * 1024 * 1024

time: 71.4 us -> 67.5 us (0.945)
  Pallas kernels: 68.8 us -> 64.9 us
    pallas_call x1, Pallas kernels: 68.8 us -> 64.9 us  [on_device(): pl.pallas_call(kernel, out_shape=(jax.ShapeDtypeStruct((512, 128), BF16),...]
where the time goes in v6:
time: 67.5 us; the launch traced here: 67.4 us
  Pallas kernels  64.9 us (96%)
  local copies, waits for them, and re-layouts  1.86 us (3%)
    pallas_call x1, Pallas kernels, on_device(): pl.pallas_call(kernel, out_shape=(jax.ShapeDtypeStruct((512, 128), BF16),...  64.9 us
    unnamed x2, local copies, waits for them, and re-layouts  1.86 us

profile of v6, /device:TPU:1, one launch (start us, length us, event | category | flops | bytes accessed | tf_op | source)
XLA Modules:
  0.0 67.4 jit_solution(2329954315674102524)
XLA Ops:
  0.6 64.9 %shard_map.77 = (bf16[512,128]{1,0:T(8,128)(2,1)S(1)}, bf16[2,27,2,64,128]{4,3,2,1,0:T(8,128)(2,1)S(1)}) custom-call(bf16[512,128]{1,0:T(8,128)(2,1)} %bitcast.10, bf16[2,512,128]{2,1,0:T(8,128)(2,1)} %bitcast.9, bf16[512,128]{1,0:T(8,128)(2,1)} %bitcast.11, s32[1,512]{1,0:T(1,128)} %bitcast.12, s32[1,27]{1,0:T(1,128)} %bitcast.13, ...), custom_call_target="tpu_custom_call" | custom-call | flops 2000000000 | bytes 5000000 | tf_op jit(solution)/shard_map/pallas_call | solution.py:458
  65.5 0.7 copy.10
  66.2 1.2 %copy.11 = bf16[2,27,128,128]{3,2,1,0:T(8,128)(2,1)} copy(bf16[2,27,128,128]{3,2,1,0:T(8,128)(2,1)S(1)} %bitcast.7) | data formatting | bytes 3538944

commit v7 on v6

--- a/solution.py
+++ b/solution.py
@@ -26,8 +26,8 @@
     plane_me = x * 4 + y
     z_me = z_hi * 4 + z_lo
 
-    def plane_device(i):
-        return {"gx": z_hi * 4 + i // 4, "gy": (i % 4) * 8 + z_lo * 2 + core}
+    def plane_device(i, j):
+        return {"gx": z_hi * 4 + i, "gy": j * 8 + z_lo * 2 + core}
 
     def z_device(i):
         return {"gx": (i // 4) * 4 + x, "gy": y * 8 + (i % 4) * 2 + core}
@@ -36,6 +36,8 @@
 
     def side_device(a, b):
         return {"gx": (gx + a + 16) % 16, "gy": (gy + b + 32) % 32}
+
+    xs, ys = [(x + d) % 4 for d in range(4)], [(y + d) % 4 for d in range(4)]
 
     def plane_shift(i):
         v = i + i // 10
@@ -43,11 +45,11 @@
 
     def plane_to(i):
         dx, dy = plane_shift(i)
-        return ((x + dx) % 4) * 4 + (y + dy) % 4
+        return xs[dx] * 4 + ys[dy]
 
     def plane_from(i):
         dx, dy = plane_shift(i)
-        return ((x + 4 - dx) % 4) * 4 + (y + 4 - dy) % 4
+        return xs[-dx] * 4 + ys[-dy]
 
     def z_far(i):
         return 8 + (i // 2) - (i % 2) * (2 * (i // 2) + 1)
@@ -79,11 +81,9 @@
     for shift in (1, 15):
         greet(barrier, z_device((z_me + shift) % 16))
 
-    def greet_plane(i, carry):
-        greet(barrier, plane_device(plane_to(i)))
-        return carry
-
-    lax.fori_loop(0, 15, greet_plane, 0)
+    for i in range(15):
+        dx, dy = plane_shift(i)
+        greet(barrier, plane_device(xs[dx], ys[dy]))
     w_copies = [pltpu.make_async_copy(w_any.at[l], wv.at[l], wsem.at[l]) for l in (1, 0)]
     for copy in w_copies:
         copy.start()
@@ -196,11 +196,11 @@
 
     def plane_copy(b, i):
         l, _, chunk, _ = BATCHES[b]
-        peer = plane_to(i)
+        peer, (dx, dy) = plane_to(i), plane_shift(i)
         return pltpu.make_async_remote_copy(
             src_ref=psend.at[l, part(b, peer)], dst_ref=precv.at[b, i, pl.ds(0, chunk)],
             send_sem=pss.at[b], recv_sem=prs.at[b],
-            device_id=plane_device(peer), device_id_type=MESH,
+            device_id=plane_device(xs[dx], ys[dy]), device_id_type=MESH,
         )
 
     def z_copy(b, o):
@@ -237,10 +237,11 @@
     def plane_back(b, i):
         l = BATCHES[b][0]
         rows = part(b, plane_me)
+        dx, dy = plane_shift(i)
         return pltpu.make_async_remote_copy(
             src_ref=ag.at[l, core, rows], dst_ref=ag.at[l, core, rows],
             send_sem=pas.at[b], recv_sem=par.at[b, i],
-            device_id=plane_device(plane_to(i)), device_id_type=MESH,
+            device_id=plane_device(xs[dx], ys[dy]), device_id_type=MESH,
         )
 
     def core_back(b, owner):
@@ -253,11 +254,8 @@
         )
 
     def each(first, last, act):
-        def step(j, carry):
+        for j in range(first, last):
             act(j)
-            return carry
-
-        lax.fori_loop(first, last, step, 0)
 
     def sum_halves(b):
         l = BATCHES[b][0]
@@ -279,12 +277,11 @@
     def sum_plane(b):
         l, _, chunk, _ = BATCHES[b]
 
-        def add(i, total):
-            return total + precv[b, i, pl.ds(0, chunk)].astype(F32)
-
         plane_all(b).wait_recv()
         rows = part(b, plane_me)
-        total = lax.fori_loop(0, 15, add, s[l, core, rows] + crecv[l, rows])
+        total = s[l, core, rows] + crecv[l, rows]
+        for i in range(15):
+            total = total + precv[b, i, :chunk].astype(F32)
         zsend[b, : chunk // 16] = total.reshape(chunk // 16, 16, 128).astype(BF16)
 
         def send(o):
@@ -299,12 +296,10 @@
         def _():
             o = z_hi
 
-            def add(i, total):
-                return total + zrecv[b, i].astype(F32)
-
             z_all(b).wait_recv()
-
-            total = lax.fori_loop(0, 15, add, zsend[b, o].astype(F32))
+            total = zsend[b, o].astype(F32)
+            for i in range(15):
+                total = total + zrecv[b, i].astype(F32)
             zfin[b, o] = (total * (1.0 / 512.0)).astype(BF16)
             each(0, 15, lambda i: z_back(b, i, o).start())
 

time: 67.5 us -> 66.3 us (0.982)
  Pallas kernels: 64.9 us -> 63.7 us
    pallas_call x1, Pallas kernels: 64.9 us -> 63.7 us  [on_device(): pl.pallas_call(kernel, out_shape=(jax.ShapeDtypeStruct((512, 128), BF16),...]
where the time goes in v7:
time: 66.3 us; the launch traced here: 66.2 us
  Pallas kernels  63.7 us (96%)
  local copies, waits for them, and re-layouts  1.86 us (3%)
    pallas_call x1, Pallas kernels, on_device(): pl.pallas_call(kernel, out_shape=(jax.ShapeDtypeStruct((512, 128), BF16),...  63.7 us
    unnamed x2, local copies, waits for them, and re-layouts  1.86 us

profile of v7, /device:TPU:1, one launch (start us, length us, event | category | flops | bytes accessed | tf_op | source)
XLA Modules:
  0.0 66.2 jit_solution(942380746990486046)
XLA Ops:
  0.6 63.7 %shard_map.77 = (bf16[512,128]{1,0:T(8,128)(2,1)S(1)}, bf16[2,27,2,64,128]{4,3,2,1,0:T(8,128)(2,1)S(1)}) custom-call(bf16[512,128]{1,0:T(8,128)(2,1)} %bitcast.10, bf16[2,512,128]{2,1,0:T(8,128)(2,1)} %bitcast.9, bf16[512,128]{1,0:T(8,128)(2,1)} %bitcast.11, s32[1,512]{1,0:T(1,128)} %bitcast.12, s32[1,27]{1,0:T(1,128)} %bitcast.13, ...), custom_call_target="tpu_custom_call" | custom-call | flops 2000000000 | bytes 5000000 | tf_op jit(solution)/shard_map/pallas_call | solution.py:453
  64.3 0.7 copy.10
  65.0 1.2 %copy.11 = bf16[2,27,128,128]{3,2,1,0:T(8,128)(2,1)} copy(bf16[2,27,128,128]{3,2,1,0:T(8,128)(2,1)S(1)} %bitcast.7) | data formatting | bytes 3538944

commit v8 on v7

--- a/solution.py
+++ b/solution.py
@@ -11,12 +11,16 @@
 SIDES = [(a, b) for a in (-1, 0, 1) for b in (-1, 0, 1) if (a, b) != (0, 0)]
 BATCHES = ((1, 0, 64, 0), (1, 1024, 48, 2), (0, 0, 64, 1), (0, 1024, 48, 3))
 HALF = 27 * 64
+SHIFTS = (
+    (2, 2), (3, 1), (0, 2), (1, 3), (2, 0), (3, 2), (2, 1), (1, 2),
+    (0, 1), (3, 3), (2, 3), (1, 0), (0, 3), (1, 1), (3, 0),
+)
 
 
 def kernel(
     feat_any, pre_any, cot_any, mask_any, nbr_any, w_any, gin, wg,
     feat, pre, cot, mask, nbr, wv, maskv, pad, pg, rowsT, gface, gcorner, rface, rcorner,
-    s, crecv, psend, precv, zsend, zrecv, zfin, ag,
+    s, sent, crecv, psend, precv, zsend, zrecv, zfin, ag,
     isem, wsem, osem, hss, hrs, css, crs, pss, prs, zss, zrs, zas, zar, pas, par, cas, car, relays,
 ):
     gx, gy = lax.axis_index("gx"), lax.axis_index("gy")
@@ -40,8 +44,7 @@
     xs, ys = [(x + d) % 4 for d in range(4)], [(y + d) % 4 for d in range(4)]
 
     def plane_shift(i):
-        v = i + i // 10
-        return (2 + v // 4) % 4, (2 + v % 4) % 4
+        return SHIFTS[i]
 
     def plane_to(i):
         dx, dy = plane_shift(i)
@@ -180,6 +183,7 @@
                 for h in (0, 1):
                     at = m * 128 + q * 64
                     s[l, h, at : at + 64] = block[h * 64 : (h + 1) * 64]
+                    sent[l, h, at : at + 64] = block[h * 64 : (h + 1) * 64].astype(BF16)
 
     def part(b, i):
         _, base, chunk, _ = BATCHES[b]
@@ -189,7 +193,7 @@
         l, base, chunk, _ = BATCHES[b]
         rows = pl.ds(base, 16 * chunk)
         return pltpu.make_async_remote_copy(
-            src_ref=s.at[l, other, rows], dst_ref=crecv.at[l, rows],
+            src_ref=sent.at[l, other, rows], dst_ref=crecv.at[l, rows],
             send_sem=css.at[b], recv_sem=crs.at[b],
             device_id=core_device, device_id_type=MESH,
         )
@@ -263,7 +267,7 @@
 
         def chunk(i):
             rows = part(b, plane_to(i))
-            psend[l, rows] = (s[l, core, rows] + crecv[l, rows]).astype(BF16)
+            psend[l, rows] = (s[l, core, rows] + crecv[l, rows].astype(F32)).astype(BF16)
             plane_copy(b, i).start()
 
         each(0, 15, chunk)
@@ -279,7 +283,7 @@
 
         plane_all(b).wait_recv()
         rows = part(b, plane_me)
-        total = s[l, core, rows] + crecv[l, rows]
+        total = s[l, core, rows] + crecv[l, rows].astype(F32)
         for i in range(15):
             total = total + precv[b, i, :chunk].astype(F32)
         zsend[b, : chunk // 16] = total.reshape(chunk // 16, 16, 128).astype(BF16)
@@ -474,7 +478,8 @@
             pltpu.VMEM((3, 4, 64, 128), BF16),
             pltpu.VMEM((2, 4, 16, 128), BF16),
             pltpu.VMEM((2, 2, 28 * 64, 128), F32),
-            pltpu.VMEM((2, 28 * 64, 128), F32),
+            pltpu.VMEM((2, 2, 28 * 64, 128), BF16),
+            pltpu.VMEM((2, 28 * 64, 128), BF16),
             pltpu.VMEM((2, 28 * 64, 128), BF16),
             pltpu.VMEM((4, 15, 64, 128), BF16),
             pltpu.VMEM((4, 4, 16, 128), BF16),

time: 66.3 us -> 66 us (level)
  no operation moved by 1% of the time
where the time goes in v8:
time: 66 us; the launch traced here: 65.9 us
  Pallas kernels  63.3 us (96%)
  local copies, waits for them, and re-layouts  1.86 us (3%)
    pallas_call x1, Pallas kernels, on_device(): pl.pallas_call(kernel, out_shape=(jax.ShapeDtypeStruct((512, 128), BF16),...  63.3 us
    unnamed x2, local copies, waits for them, and re-layouts  1.86 us

profile of v8, /device:TPU:1, one launch (start us, length us, event | category | flops | bytes accessed | tf_op | source)
XLA Modules:
  0.0 65.9 jit_solution(17741218594177490992)
XLA Ops:
  0.6 63.3 %shard_map.77 = (bf16[512,128]{1,0:T(8,128)(2,1)S(1)}, bf16[2,27,2,64,128]{4,3,2,1,0:T(8,128)(2,1)S(1)}) custom-call(bf16[512,128]{1,0:T(8,128)(2,1)} %bitcast.10, bf16[2,512,128]{2,1,0:T(8,128)(2,1)} %bitcast.9, bf16[512,128]{1,0:T(8,128)(2,1)} %bitcast.11, s32[1,512]{1,0:T(1,128)} %bitcast.12, s32[1,27]{1,0:T(1,128)} %bitcast.13, ...), custom_call_target="tpu_custom_call" | custom-call | flops 2000000000 | bytes 5000000 | tf_op jit(solution)/shard_map/pallas_call | solution.py:457
  64.0 0.7 copy.10
  64.6 1.2 %copy.11 = bf16[2,27,128,128]{3,2,1,0:T(8,128)(2,1)} copy(bf16[2,27,128,128]{3,2,1,0:T(8,128)(2,1)S(1)} %bitcast.7) | data formatting | bytes 3538944
